TPU v7x, 32 devices: a whole 2x2x4 slice. The times are simulated.
32 devices in a mesh: freq: 2 (over y), tm: 16 (over z, x, core).
Axes of the slice: x: 2, y: 2, z: 4, core: 2. Of those that a mesh axis runs over, the one named last changes fastest.
Arguments:
- tokens: bfloat16 [2, 8, 1024, 768], P(None, 'freq', 'tm'), may hold values from -6 to 6
- out_grad: bfloat16 [2, 8, 1024, 768], P(None, 'freq', 'tm'), may hold values from -6 to 6
- lengths: int32 [2], replicated, may hold values from 128 to 1024, as said below
- norm1_gain: float32 [768], replicated, may hold values from 0.1 to 1.9
- norm1_shift: float32 [768], replicated, may hold values from -1.75 to 1.75
- w_qkv: bfloat16 [768, 2304], replicated, may hold values from -0.21875 to 0.21875
- query_bias: float32 [768], replicated, may hold values from -3 to 3
- value_bias: float32 [768], replicated, may hold values from -0.125 to 0.125
- w_proj: bfloat16 [768, 768], replicated, may hold values from -6 to 6
- proj_bias: float32 [768], replicated, may hold values from -1.75 to 1.75
- norm2_gain: float32 [768], replicated, may hold values from 0.1 to 1.9
- norm2_shift: float32 [768], replicated, may hold values from -1.75 to 1.75
- w_fc1: bfloat16 [768, 3072], replicated, may hold values from -0.21875 to 0.21875
- fc1_bias: float32 [3072], replicated, may hold values from -3 to 3
- w_fc2: bfloat16 [3072, 768], replicated, may hold values from -0.109375 to 0.109375
- fc2_bias: float32 [768], replicated, may hold values from -1.75 to 1.75
- moment: float32 [7090176], P(('freq', 'tm'))
- ema_decay: float32 [1], replicated, may hold values from 0.5 to 0.95
Outputs:
- mixed: bfloat16 [2, 8, 1024, 768], P(None, 'freq', 'tm')
- input_grad: bfloat16 [2, 8, 1024, 768], P(None, 'freq', 'tm')
- weight_grad: float32 [7090176], P(('freq', 'tm'))
- new_moment: float32 [7090176], P(('freq', 'tm'))
Inputs may be any that keep to these rules, and one draw needn't show every extreme that they name: `lengths`: at least one clip slot, drawn from the seed, is 1024 frames long.
All inputs are finite; a program needn't handle non-finite values.
Results may differ from a plain program's by a relative error of at most 0.013.
Values may be sent and summed in bfloat16 or wider, within the bound.
No kernel may reach another device: no remote copies, remote signals or barrier semaphores. Data moves between devices by JAX's collectives and lax.ppermute only.
A program may use at most 512 MiB of HBM per device.

v0:
```python
import functools
import math

import jax
import jax.numpy as jnp
from jax import lax
from jax.experimental import pallas as pl
from jax.experimental.pallas import tpu as pltpu
from jax.sharding import Mesh
from jax.sharding import PartitionSpec as P

HEADS = 12
HEAD_DIM = 64
GROUPS = 4
GROUP_HEADS = HEADS // GROUPS
PAIR = 2 * HEAD_DIM
LANES = 128
OUT_ROWS = HEAD_DIM + 8
GRAD_ROWS = HEAD_DIM + 16
EPSILON = 1e-06
NEGATIVE = -1e30
LOG2E = math.log2(math.e)
LN2 = math.log(2.0)
SCALE = HEAD_DIM**-0.5
VMEM_LIMIT = 60 * 2**20
BF16 = jnp.bfloat16
F32 = jnp.float32


TOKEN = jax.ShapeDtypeStruct((8, LANES), F32)
TOKEN_SPEC = pl.BlockSpec((8, LANES), lambda i, *_: (0, 0))


def dot32(left, right, contract):
    return lax.dot_general(left, right, ((contract[:1], contract[1:]), ((), ())), preferred_element_type=F32)


def work(info_ref, clip, times, frames):
    t, full, rest = info_ref[0], info_ref[1 + clip] // frames, info_ref[1 + clip] % frames
    live = full + (rest > 0).astype(jnp.int32)
    query_blocks = (live + times - 1) // times
    key_blocks = jnp.maximum(full - t + times - 1, 0) // times
    partial = (rest > 0) & (full % times == t)
    return query_blocks, key_blocks, partial, rest


def joined(ref, late):
    tiles = [ref[late, j] for j in range(ref.shape[1])]
    return tiles[0] if len(tiles) == 1 else jnp.concatenate(tiles, axis=1)


def load_pairs(kv_refs, slot):
    return [ref[f, slot, 0] for ref in kv_refs for f in range(ref.shape[0])]


def attend_kernel(clip, times, frames, n_kv, n_q, n_out, info_ref, *refs):
    kv_refs, q_refs, refs = refs[:n_kv], refs[n_kv : n_kv + n_q], refs[n_kv + n_q :]
    refs = refs[-n_out - 6 :]
    out_refs, (token_ref, acc, top, q_pad, scores, tops) = refs[:n_out], refs[n_out:]
    token_ref[...] = jnp.zeros_like(token_ref)
    query_blocks, key_blocks, partial, rest = work(info_ref, clip, times, frames)
    width = q_refs[0].shape[1] * q_refs[0].shape[3]
    rows = scores.shape[1]
    for late in range(GROUPS):
        for p, ref in enumerate(q_refs):
            q_pad[late, :HEAD_DIM, p * width : (p + 1) * width] = joined(ref, late)
        q_pad[late, HEAD_DIM:, :] = jnp.zeros((HEAD_DIM, q_pad.shape[2]), BF16)
    acc[...] = jnp.zeros_like(acc)
    top[...] = jnp.full_like(top, NEGATIVE)
    ones = jnp.ones((16, rows), BF16)

    def load(block):
        return jnp.concatenate(load_pairs(kv_refs, block), axis=0)

    def consume(u, pair, block_scores, block_top):
        old = top[u]
        new = jnp.maximum(old, block_top)
        probs = jnp.exp2(block_scores - new).astype(BF16)
        top[u] = new
        values = jnp.concatenate([pair.T[HEAD_DIM:], ones], axis=0)
        acc[u] = acc[u] * jnp.exp2(old - new) + dot32(values, probs, (1, 0))

    def masked(u, _):
        pair = load(key_blocks)
        alive = lax.broadcasted_iota(jnp.int32, (rows, 1), 0) % frames < rest
        block_scores = jnp.where(alive, dot32(pair, q_pad[u], (1, 0)), NEGATIVE)
        consume(u, pair, block_scores, jnp.max(block_scores, axis=0, keepdims=True))
        return 0

    lax.fori_loop(0, jnp.where(partial, query_blocks, 0), masked, 0)
    total = query_blocks * key_blocks
    per = jnp.maximum(key_blocks, 1)

    def score(step, slot):
        block_scores = dot32(load(step % per), q_pad[step // per], (1, 0))
        scores[slot] = block_scores
        tops[slot] = jnp.max(block_scores, axis=0, keepdims=True)

    @pl.when(total > 0)
    def _():
        score(0, 0)

    def two_steps(double, _):
        for slot in range(2):
            step = 2 * double + slot
            score(jnp.minimum(step + 1, total - 1), 1 - slot)
            consume(step // per, load(step % per), scores[slot], tops[slot])
        return 0

    lax.fori_loop(0, total // 2, two_steps, 0)

    @pl.when(total % 2 == 1)
    def _():
        consume((total - 1) // per, load((total - 1) % per), scores[0], tops[0])

    for late in range(GROUPS):
        norm = acc[late, HEAD_DIM : HEAD_DIM + 1, :]
        some = norm > 0.0
        safe = jnp.where(some, norm, 1.0)
        out = acc[late, :HEAD_DIM, :] / safe
        lse = jnp.where(some, top[late] + jnp.log2(safe), NEGATIVE)
        fill = jnp.zeros((GRAD_ROWS - HEAD_DIM - 3, out.shape[1]), F32)
        full = jnp.concatenate([out, thirds(lse), fill], axis=0).astype(BF16)
        for p, ref in enumerate(out_refs):
            ref[late] = full[:, p * width : (p + 1) * width]


def specs_of(kv, q, place, places):
    kv_specs = [pl.BlockSpec((a.shape[0], GROUPS, 1, *a.shape[3:]), lambda i, *_: (0, 0, place, 0, 0)) for a in kv]
    _, tiles, _, lanes = q[0].shape
    q_specs = [pl.BlockSpec((GROUPS, tiles // places, HEAD_DIM, lanes), lambda i, *_: (0, place, 0, 0)) for a in q]
    return kv_specs, q_specs, tiles * lanes // places


def attend(info, kv, q, place, clip, clips, times, frames, before, after):
    kv_specs, q_specs, width = specs_of(kv, q, place, kv[0].shape[2])
    queries = len(q) * width
    rows = sum(a.shape[0] for a in kv) * kv[0].shape[3]
    pairs = GROUPS * rows * GROUPS * queries
    out_specs = [pl.BlockSpec((GROUPS, GRAD_ROWS, width), lambda i, *_: (0, 0, clip % clips))] * len(q) + [TOKEN_SPEC]
    n_in = 1 + len(kv) + len(q)
    return pl.pallas_call(
        functools.partial(attend_kernel, clip, times, frames, len(kv), len(q), len(q)),
        grid_spec=pltpu.PrefetchScalarGridSpec(
            num_scalar_prefetch=1,
            grid=(1,),
            in_specs=kv_specs + q_specs + [pl.BlockSpec(memory_space=pl.ANY)] * (len(before) + len(after)),
            out_specs=out_specs,
            scratch_shapes=[
                pltpu.VMEM((GROUPS, GRAD_ROWS, queries), F32),
                pltpu.VMEM((GROUPS, 1, queries), F32),
                pltpu.VMEM((GROUPS, PAIR, queries), BF16),
                pltpu.VMEM((2, rows, queries), F32),
                pltpu.VMEM((2, 1, queries), F32),
            ],
        ),
        out_shape=[jax.ShapeDtypeStruct((GROUPS, GRAD_ROWS, clips * width), BF16)] * len(q) + [TOKEN],
        input_output_aliases={n_in + i: i for i in range(len(before))},
        compiler_params=pltpu.CompilerParams(vmem_limit_bytes=VMEM_LIMIT),
        cost_estimate=pl.CostEstimate(flops=256 * pairs, bytes_accessed=pairs // 16, transcendentals=pairs),
    )(info, *kv, *q, *before, *after)


def attend_back_kernel(clip, times, frames, cuts, n_kv, n_q, n_out, info_ref, *refs):
    kv_refs, q_refs, grad_refs = refs[:n_kv], refs[n_kv : n_kv + n_q], refs[n_kv + n_q : n_kv + 2 * n_q]
    refs = refs[-n_out - n_kv - 7 :]
    back_q_refs, back_kv_refs, refs = refs[:n_out], refs[n_out : n_out + n_kv], refs[n_out + n_kv :]
    refs[0][...] = jnp.zeros_like(refs[0])
    _, back_q, back_kv, q_cols, grad_cols, lse, delta = refs
    query_blocks, key_blocks, partial, rest = work(info_ref, clip, times, frames)
    width = grad_refs[0].shape[-1]
    part_rows = kv_refs[0].shape[3]
    rows = back_kv.shape[1]
    cut = rows // cuts
    zero = jnp.zeros((HEAD_DIM, width), BF16)

    def prepare(late, _):
        for p, (q_ref, grad_ref) in enumerate(zip(q_refs, grad_refs)):
            cols = slice(p * width, (p + 1) * width)
            q_cols[late, :, cols] = jnp.concatenate([joined(q_ref, late), zero], axis=0)
            grad_cols[late, :, cols] = jnp.concatenate([zero, grad_ref[late, :HEAD_DIM]], axis=0)
            extra = grad_ref[late, HEAD_DIM:].astype(F32)
            lse[late, :, cols] = extra[0:1] + extra[1:2] + extra[2:3]
            delta[late, :, cols] = extra[3:4] + extra[4:5] + extra[5:6]
        return 0

    lax.fori_loop(0, query_blocks, prepare, 0)
    back_q[...] = jnp.zeros_like(back_q)
    back_kv[...] = jnp.zeros_like(back_kv)

    def step(u, block, masked):
        pairs = load_pairs(kv_refs, block)
        for k in range(cuts):
            part = pairs[k * len(pairs) // cuts : (k + 1) * len(pairs) // cuts]
            pair = part[0] if len(part) == 1 else jnp.concatenate(part, axis=0)
            probs = jnp.exp2(dot32(pair, q_cols[u], (1, 0)) - lse[u])
            if masked:
                row = lax.broadcasted_iota(jnp.int32, (cut, 1), 0)
                probs = jnp.where(row % frames < rest, probs, 0.0)
            back_probs = dot32(pair, grad_cols[u], (1, 0))
            back_scores = (probs * (back_probs - delta[u])).astype(BF16)
            back_pair = dot32(probs.astype(BF16), grad_cols[u], (1, 1)) + dot32(back_scores, q_cols[u], (1, 1))
            back_q[u] += dot32(pair, back_scores, (0, 0))
            back_kv[block, k * cut : (k + 1) * cut, :] += back_pair
        return 0

    lax.fori_loop(0, jnp.where(partial, query_blocks, 0), lambda u, _: step(u, key_blocks, True), 0)
    per = jnp.maximum(key_blocks, 1)
    lax.fori_loop(0, query_blocks * key_blocks, lambda i, _: step(i // per, i % per, False), 0)
    is_key = lax.broadcasted_iota(jnp.int32, (1, PAIR), 1) < HEAD_DIM
    factor = jnp.where(is_key, jnp.float32(LN2), jnp.float32(1.0))
    for late in range(GROUPS):
        for p, ref in enumerate(back_q_refs):
            ref[late] = (back_q[late, :HEAD_DIM, p * width : (p + 1) * width] * SCALE).astype(BF16)
        p = 0
        for ref in back_kv_refs:
            for f in range(ref.shape[0]):
                ref[f, late, 0] = (back_kv[late, p * part_rows : (p + 1) * part_rows, :] * factor).astype(BF16)
                p += 1


def attend_back(info, kv, q, grad, place, clip, clips, times, frames, before, after):
    kv_specs, q_specs, width = specs_of(kv, q, place, kv[0].shape[2])
    queries = len(q) * width
    rows = sum(a.shape[0] for a in kv) * kv[0].shape[3]
    pairs = GROUPS * rows * GROUPS * queries
    grad_specs = [pl.BlockSpec((GROUPS, GRAD_ROWS, width), lambda i, *_: (0, 0, clip)) for a in grad]
    q_out = [pl.BlockSpec((GROUPS, HEAD_DIM, width), lambda i, *_: (0, 0, clip % clips))] * len(q)
    kv_out = [pl.BlockSpec((a.shape[0], GROUPS, 1, *a.shape[3:]), lambda i, *_: (0, 0, clip % clips, 0, 0)) for a in kv]
    n_in = 1 + len(kv) + len(q) + len(grad)
    return pl.pallas_call(
        functools.partial(attend_back_kernel, clip, times, frames, 2, len(kv), len(q), len(q)),
        grid_spec=pltpu.PrefetchScalarGridSpec(
            num_scalar_prefetch=1,
            grid=(1,),
            in_specs=kv_specs + q_specs + grad_specs + [pl.BlockSpec(memory_space=pl.ANY)] * (len(before) + len(after)),
            out_specs=q_out + kv_out + [TOKEN_SPEC],
            scratch_shapes=[
                pltpu.VMEM((GROUPS, PAIR, queries), F32),
                pltpu.VMEM((GROUPS, rows, PAIR), F32),
                pltpu.VMEM((GROUPS, PAIR, queries), BF16),
                pltpu.VMEM((GROUPS, PAIR, queries), BF16),
                pltpu.VMEM((GROUPS, 1, queries), F32),
                pltpu.VMEM((GROUPS, 1, queries), F32),
            ],
        ),
        out_shape=[jax.ShapeDtypeStruct((GROUPS, HEAD_DIM, clips * width), BF16)] * len(q)
        + [jax.ShapeDtypeStruct((a.shape[0], GROUPS, clips, *a.shape[3:]), BF16) for a in kv]
        + [TOKEN],
        input_output_aliases={n_in + i: i for i in range(len(before))},
        compiler_params=pltpu.CompilerParams(vmem_limit_bytes=VMEM_LIMIT),
        cost_estimate=pl.CostEstimate(flops=640 * pairs, bytes_accessed=pairs // 8, transcendentals=pairs),
    )(info, *kv, *q, *grad, *before, *after)


def thirds(values):
    high = values.astype(BF16).astype(F32)
    middle = (values - high).astype(BF16).astype(F32)
    return jnp.concatenate([high, middle, values - high - middle], axis=0)


def merge_kernel(_, *refs):
    part_refs, (out_ref, low_ref) = refs[:-2], refs[-2:]
    for n in range(GROUPS):
        parts = [ref[n].astype(F32) for ref in part_refs]
        lses = [p[HEAD_DIM : HEAD_DIM + 1] + p[HEAD_DIM + 1 : HEAD_DIM + 2] + p[HEAD_DIM + 2 : HEAD_DIM + 3] for p in parts]
        most = functools.reduce(jnp.maximum, lses)
        shares = [jnp.exp2(lse - most) for lse in lses]
        total = sum(shares)
        out = sum(p[:HEAD_DIM] * share for p, share in zip(parts, shares)) / total
        low_ref[n] = out.astype(BF16)
        out_ref[n, :HEAD_DIM] = out
        out_ref[n, HEAD_DIM:] = jnp.broadcast_to(most + jnp.log2(total), (OUT_ROWS - HEAD_DIM, out.shape[1]))


def merge(parts, after):
    _, _, width = parts[0].shape
    return pl.pallas_call(
        merge_kernel,
        in_specs=[pl.BlockSpec(memory_space=pl.ANY)] + [pl.BlockSpec(memory_space=pltpu.VMEM)] * len(parts),
        out_shape=[jax.ShapeDtypeStruct((GROUPS, OUT_ROWS, width), F32), jax.ShapeDtypeStruct((GROUPS, HEAD_DIM, width), BF16)],
        compiler_params=pltpu.CompilerParams(vmem_limit_bytes=VMEM_LIMIT),
    )(after, *parts)


def grad_rows_kernel(n_out, grad_ref, *refs):
    out_refs, ready_refs = refs[:n_out], refs[-GROUP_HEADS:]
    for head in range(GROUP_HEADS):
        for n in range(GROUPS):
            grad = grad_ref[n, head * HEAD_DIM : (head + 1) * HEAD_DIM].astype(F32)
            out = out_refs[head][n]
            if head == GROUP_HEADS - 1 and n_out > GROUP_HEADS:
                out = jnp.concatenate([ref[n] for ref in out_refs[head:]], axis=1)
            delta = jnp.sum(grad * out[:HEAD_DIM], axis=0, keepdims=True)
            fill = jnp.zeros((GRAD_ROWS - HEAD_DIM - 6, grad.shape[1]), F32)
            rows = jnp.concatenate([grad, thirds(out[HEAD_DIM : HEAD_DIM + 1]), thirds(delta), fill], axis=0)
            ready_refs[head][n] = rows.astype(BF16)


def grad_rows_of(grad, outs, after):
    width = grad.shape[-1]
    whole = pl.BlockSpec(memory_space=pltpu.VMEM)
    return pl.pallas_call(
        functools.partial(grad_rows_kernel, len(outs)),
        in_specs=[whole] * (1 + len(outs)) + [pl.BlockSpec(memory_space=pl.ANY)],
        out_shape=[jax.ShapeDtypeStruct((GROUPS, GRAD_ROWS, width), BF16)] * GROUP_HEADS,
        compiler_params=pltpu.CompilerParams(vmem_limit_bytes=VMEM_LIMIT),
    )(grad, *outs, after)


def sum_back_kernel(_, kept_ref, came_ref, *refs):
    q_refs, ready_ref = refs[:-1], refs[-1]
    rows = kept_ref.shape[1]
    for n in range(GROUPS):
        ready_ref[n, :rows] = (kept_ref[n].astype(F32) + came_ref[n].astype(F32)).astype(BF16)
        query = sum(ref[n].astype(F32) for ref in q_refs).astype(BF16)
        for j in range(rows // LANES):
            at = rows + j * HEAD_DIM
            ready_ref[n, at : at + HEAD_DIM] = query[:, j * LANES : (j + 1) * LANES]


def sum_back(after, kept, came, queries):
    groups, rows, _ = kept.shape
    return pl.pallas_call(
        sum_back_kernel,
        in_specs=[pl.BlockSpec(memory_space=pl.ANY)] + [pl.BlockSpec(memory_space=pltpu.VMEM)] * (2 + len(queries)),
        out_shape=jax.ShapeDtypeStruct((groups, rows + rows // LANES * HEAD_DIM, LANES), BF16),
        compiler_params=pltpu.CompilerParams(vmem_limit_bytes=VMEM_LIMIT),
    )(after, kept, came, *queries)


def spread(lines, at, stride, values):
    rows, width = values.shape
    for piece in range(width // LANES):
        lines[pl.ds(at + piece, rows, stride=stride), :] = values[:, piece * LANES : (piece + 1) * LANES]


def write_window(start, lines, ref, at=0):
    skip = start % 8
    rows = ref.shape[1]
    base = pl.multiple_of(start - skip, 8)
    for s in range(8):

        @pl.when(skip == s)
        def _():
            ref[at] = lines[pl.ds(base, rows + 8), :][s : s + rows].astype(BF16)


def pack_early_kernel(size, first, att_ref, branch_ref, normed_ref, pre_ref, act_ref, out_ref, vec_ref, window_ref, lines):
    step = pl.program_id(0)

    @pl.when(step == 0)
    def _():
        width = branch_ref.shape[1]
        blocks = pre_ref.shape[1] // width
        per = width // LANES
        spread(lines, 0, per, dot32(att_ref[...], branch_ref[...], (1, 0)))
        at = width * per
        lines[at : at + 3 * per, :] = vec_ref[0 : 3 * per]
        at += 3 * per
        for b in range(blocks):
            cols = slice(b * width, (b + 1) * width)
            spread(lines, at + b * per, blocks * per, dot32(normed_ref[...], pre_ref[:, cols], (0, 0)))
        at += blocks * width * per
        lines[at : at + blocks * per, :] = vec_ref[3 * per : (3 + blocks) * per]
        at += blocks * per
        for b in range(blocks):
            cols = slice(b * width, (b + 1) * width)
            spread(lines, at + b * width * per, per, dot32(act_ref[:, cols], out_ref[...], (0, 0)))
        at += blocks * width * per
        lines[at : at + per, :] = vec_ref[(3 + blocks) * per :]
        lines[at + per :, :] = jnp.zeros((lines.shape[0] - at - per, LANES), F32)

    @pl.when(step < first)
    def _():
        window_ref[...] = jnp.zeros_like(window_ref)

    @pl.when(step >= first)
    def _():
        write_window((step - first) * size, lines, window_ref)


def early_order(chunk):
    f, g, x, c = chunk // 16, chunk // 4 % 4, chunk // 2 % 2, chunk % 2
    return ((c * 2 + x) * 2 + f) * 4 + g


def pack_early(devices, size, *operands):
    chunks = devices - LATE_CHUNKS
    whole = [pl.BlockSpec(a.shape, lambda j: (0, 0)) for a in operands]
    entries = chunks * size * LANES
    return pl.pallas_call(
        functools.partial(pack_early_kernel, size, LATE_CHUNKS),
        grid=(devices,),
        in_specs=whole,
        out_specs=pl.BlockSpec((1, EARLY_WINDOW, LANES), lambda j: (early_order(j), 0, 0)),
        scratch_shapes=[pltpu.VMEM((-(-(chunks - 1) * size // 8) * 8 + EARLY_WINDOW + 8, LANES), F32)],
        out_shape=jax.ShapeDtypeStruct((devices, EARLY_WINDOW, LANES), BF16),
        compiler_params=pltpu.CompilerParams(vmem_limit_bytes=VMEM_LIMIT),
        cost_estimate=pl.CostEstimate(flops=1024 * entries, bytes_accessed=4 * entries, transcendentals=0),
    )(*operands)


SWAP = [(0, 1), (1, 0)]


def swap(values, axis):
    return lax.ppermute(values, axis, SWAP)


def add(left, right):
    return (left.astype(F32) + right.astype(F32)).astype(BF16)


def trade(values, dim, keep, axis):
    sent = lax.dynamic_index_in_dim(values, 1 - keep, dim, keepdims=False)
    kept = lax.dynamic_index_in_dim(values, keep, dim, keepdims=False)
    return add(kept, swap(sent, axis))


EARLY_WINDOW = 1744
LATE_CHUNKS = 8
LATE_WINDOW = 1792


def reduce_late(send, keep, after):
    f, x = lax.axis_index("f"), lax.axis_index("x")
    pairs = add(keep, swap(send, "c")).reshape(2, 2, 4, -1, LANES)
    first = trade(trade(pairs[:, :, :2], 1, x, "x"), 1, f, "f")
    second = trade(trade(pairs[:, :, 2:], 2, f, "f"), 1, x, "x")
    parts = along_g(jnp.stack([first[0], first[1], second[1], second[0]]))
    mine = sum(parts[n].astype(F32) for n in range(GROUPS)).astype(BF16)
    mine = hold(mine, [after])
    routes = ([(4, 0), (5, 1)], [(2, 1), (3, 0)], [(6, 1), (7, 0)])
    came = [lax.ppermute(mine, ("f", "g"), route) for route in routes]
    return jnp.concatenate([mine] + came, axis=0).astype(F32)


def own_chunk(early, late, size):
    is_late = (lax.axis_index("f") == 0) & (lax.axis_index("g") < 2)
    return jnp.where(is_late, late[: size // LANES], early[: size // LANES]).reshape(size)


def centre(values):
    centred = values - jnp.mean(values, axis=-1, keepdims=True)
    scale = lax.rsqrt(jnp.mean(centred * centred, axis=-1, keepdims=True) + EPSILON)
    return centred * scale, scale


def centre_back(grad, unit, scale):
    mean = jnp.mean(grad, axis=-1, keepdims=True)
    along = jnp.mean(grad * unit, axis=-1, keepdims=True)
    return scale * (grad - mean - unit * along)


def row(ref):
    return ref[...].reshape(1, -1)


def swap_halves(values):
    return pltpu.roll(values, HEAD_DIM, axis=1)


def start_kernel(x_ref, gain_ref, shift_ref, w_ref, query_bias_ref, value_bias_ref, *refs):
    rows, width = x_ref.shape

    def put(head, values):
        at = max(head % GROUP_HEADS - 1, 0) * rows
        refs[min(head % GROUP_HEADS, 1)][head // GROUP_HEADS, at : at + rows] = values.astype(BF16)

    unit, _ = centre(x_ref[...].astype(F32))
    normed = (unit * row(gain_ref) + row(shift_ref)).astype(BF16)
    keys = dot32(normed, w_ref[:, width : 2 * width], (1, 0))
    values = dot32(normed, w_ref[:, 2 * width :], (1, 0)) + row(value_bias_ref)
    is_key = lax.broadcasted_iota(jnp.int32, (1, PAIR), 1) < HEAD_DIM
    for j in range(HEADS // 2):
        key, value = keys[:, j * PAIR : (j + 1) * PAIR], values[:, j * PAIR : (j + 1) * PAIR]
        put(2 * j, jnp.where(is_key, key, swap_halves(value)))
        put(2 * j + 1, jnp.where(is_key, swap_halves(key), value))
    query = (dot32(normed, w_ref[:, :width], (1, 0)) + row(query_bias_ref)) * (SCALE * LOG2E)
    query = query.astype(BF16).T
    for head in range(HEADS):
        part = query[head * HEAD_DIM : (head + 1) * HEAD_DIM]
        ref = refs[min(head % GROUP_HEADS, 1)]
        first = ref.shape[1] // (rows + rows // LANES * HEAD_DIM) * rows
        first += max(head % GROUP_HEADS - 1, 0) * rows // LANES * HEAD_DIM
        for tile in range(rows // LANES):
            at = first + tile * HEAD_DIM
            ref[head // GROUP_HEADS, at : at + HEAD_DIM] = part[:, tile * LANES : (tile + 1) * LANES]


def one_step(kernel, info, operands, shapes, scratch, flops):
    scalars = [] if info is None else [info]
    return pl.pallas_call(
        kernel,
        grid_spec=pltpu.PrefetchScalarGridSpec(
            num_scalar_prefetch=len(scalars),
            grid=(1,),
            in_specs=[pl.BlockSpec(a.shape, lambda i, *_, n=a.ndim: (0,) * n) for a in operands],
            out_specs=[pl.BlockSpec(a.shape, lambda i, *_, n=len(a.shape): (0,) * n) for a in shapes],
            scratch_shapes=scratch,
        ),
        out_shape=shapes,
        compiler_params=pltpu.CompilerParams(vmem_limit_bytes=VMEM_LIMIT),
        cost_estimate=pl.CostEstimate(flops=flops, bytes_accessed=flops // 500, transcendentals=0),
    )(*scalars, *operands)


def start(x, gain, shift, w_qkv, query_bias, value_bias):
    rows, width = x.shape
    height = rows + rows // LANES * HEAD_DIM
    shapes = [jax.ShapeDtypeStruct((GROUPS, n * height, LANES), BF16) for n in (1, GROUP_HEADS - 1)]
    operands = (x, gain, shift, w_qkv, query_bias, value_bias)
    return one_step(start_kernel, None, operands, shapes, [], 2 * rows * width * 3 * width)


def middle_kernel(
    x_ref, out_grad_ref, keep_ref, w_proj_ref, proj_bias_ref, gain_ref, shift_ref, w_fc1_ref, fc1_bias_ref, w_fc2_ref,
    fc2_bias_ref, *refs,
):
    attended_refs, refs = refs[: GROUP_HEADS + 1], refs[GROUP_HEADS + 1 :]
    mixed_ref, back_hidden_ref, att_ref, branch_ref, normed_ref, pre_ref, act_ref, out_ref, vec_ref = refs[:9]
    grad_ref, heads = refs[9:]
    width = x_ref.shape[1]
    rows = x_ref.shape[0]
    per = width // LANES
    for head in range(HEADS):
        group, place = head // GROUP_HEADS, head % GROUP_HEADS
        if place < GROUP_HEADS - 1:
            heads[head] = attended_refs[place][group]
        else:
            heads[head, :, : rows // 2] = attended_refs[place][group]
            heads[head, :, rows // 2 :] = attended_refs[place + 1][group]
    attended = heads[...].reshape(width, rows)
    att_ref[...] = attended
    keep = keep_ref[...]
    hidden = x_ref[...].astype(F32) + (dot32(attended, w_proj_ref[...], (0, 0)) + row(proj_bias_ref))
    unit, scale = centre(hidden)
    normed = (unit * row(gain_ref) + row(shift_ref)).astype(BF16)
    normed_ref[...] = normed
    grad_out = out_grad_ref[...].astype(F32) * keep
    low_out = grad_out.astype(BF16)
    out_ref[...] = low_out
    branch2 = jnp.zeros((rows, width), F32)
    back_normed = jnp.zeros((rows, width), F32)

    def put(at, line):
        for piece in range(line.shape[1] // LANES):
            vec_ref[at + piece : at + piece + 1, :] = line[:, piece * LANES : (piece + 1) * LANES]

    blocks = pre_ref.shape[1] // width
    for b in range(blocks):
        cols = slice(b * width, (b + 1) * width)
        pre = dot32(normed, w_fc1_ref[:, cols], (1, 0)) + row(fc1_bias_ref)[:, cols]
        share = 0.5 * (1.0 + lax.erf(pre * (0.5**0.5)))
        low_act = (pre * share).astype(BF16)
        act_ref[:, cols] = low_act
        branch2 += dot32(low_act, w_fc2_ref[cols, :], (1, 0))
        slope = share + pre * jnp.exp(-0.5 * pre * pre) * ((2.0 * math.pi) ** -0.5)
        back_pre = (dot32(low_out, w_fc2_ref[cols, :], (1, 1)) * slope).astype(BF16)
        pre_ref[:, cols] = back_pre
        put((3 + b) * per, jnp.sum(back_pre.astype(F32), axis=0, keepdims=True))
        back_normed += dot32(back_pre, w_fc1_ref[:, cols], (1, 1))
    mixed_ref[...] = ((hidden + (branch2 + row(fc2_bias_ref))) * keep).astype(BF16)
    put((3 + blocks) * per, jnp.sum(low_out.astype(F32), axis=0, keepdims=True))
    put(per, jnp.sum(back_normed * unit, axis=0, keepdims=True))
    put(2 * per, jnp.sum(back_normed, axis=0, keepdims=True))
    back_hidden = grad_out + centre_back(back_normed * row(gain_ref), unit, scale)
    back_hidden_ref[...] = back_hidden
    branch = back_hidden.astype(BF16)
    branch_ref[...] = branch
    put(0, jnp.sum(branch.astype(F32), axis=0, keepdims=True))
    back_attended = dot32(w_proj_ref[...], branch, (1, 1)).astype(BF16)
    grad_ref[...] = back_attended.reshape(grad_ref.shape)


def middle(x, out_grad, keep, w_proj, proj_bias, gain, shift, w_fc1, fc1_bias, w_fc2, fc2_bias, attended):
    rows, width = x.shape
    ff = w_fc1.shape[1]
    low = lambda *shape: jax.ShapeDtypeStruct(shape, BF16)
    shapes = [
        low(rows, width), jax.ShapeDtypeStruct((rows, width), F32), low(width, rows), low(rows, width), low(rows, width),
        low(rows, ff), low(rows, ff), low(rows, width), jax.ShapeDtypeStruct(((4 * width + ff) // LANES, LANES), F32),
        low(GROUPS, width // GROUPS, rows),
    ]
    operands = [x, out_grad, keep, w_proj, proj_bias, gain, shift, w_fc1, fc1_bias, w_fc2, fc2_bias]
    operands += attended
    scratch = [pltpu.VMEM((HEADS, HEAD_DIM, rows), BF16)]
    outs = one_step(middle_kernel, None, operands, shapes, scratch, 2 * rows * width * (2 * width + 4 * ff))
    return outs[0], outs[1], outs[2:9], outs[9]


def finish_kernel(size, info_ref, x_ref, gain_ref, shift_ref, w_ref, back_hidden_ref, *refs):
    back_refs, (input_ref, send_ref, keep_ref, queries, flat, lines) = refs[: GROUP_HEADS + 1], refs[GROUP_HEADS + 1 :]
    rows, width = x_ref.shape
    per = width // LANES

    def parts_of(head):
        place = head % GROUP_HEADS
        return back_refs[place : place + 1] if place < GROUP_HEADS - 1 else back_refs[place:]

    def pair(head):
        refs = parts_of(head)
        parts = [ref[head // GROUP_HEADS, : rows // len(refs)] for ref in refs]
        return (parts[0] if len(refs) == 1 else jnp.concatenate(parts, axis=0)).astype(F32)

    for head in range(HEADS):
        refs = parts_of(head)
        tiles = rows // LANES // len(refs)
        for tile in range(rows // LANES):
            at = rows // len(refs) + tile % tiles * HEAD_DIM
            part = refs[tile // tiles][head // GROUP_HEADS, at : at + HEAD_DIM]
            queries[head, :, tile * LANES : (tile + 1) * LANES] = part
    is_key = lax.broadcasted_iota(jnp.int32, (1, PAIR), 1) < HEAD_DIM
    for j in range(HEADS // 2):
        first, second = pair(2 * j), pair(2 * j + 1)
        flat[:, j * PAIR : (j + 1) * PAIR] = jnp.where(is_key, first, swap_halves(second)).astype(BF16)
        flat[:, width + j * PAIR : width + (j + 1) * PAIR] = jnp.where(is_key, swap_halves(first), second).astype(BF16)
    query = queries[...].reshape(width, rows)
    unit, scale = centre(x_ref[...].astype(F32))
    normed = (unit * row(gain_ref) + row(shift_ref)).astype(BF16)
    spread(lines, 2 * per, 3 * per, dot32(normed, query, (0, 1)))
    for b in range(2):
        spread(lines, (3 + b) * per, 3 * per, dot32(normed, flat[:, b * width : (b + 1) * width], (0, 0)))
    back_normed = dot32(query, w_ref[:, :width], (0, 1)) + dot32(flat[...], w_ref[:, width:], (1, 1))
    input_ref[...] = (back_hidden_ref[...] + centre_back(back_normed * row(gain_ref), unit, scale)).astype(BF16)

    def put(at, line):
        for piece in range(per):
            lines[at + piece : at + piece + 1, :] = line[:, piece * LANES : (piece + 1) * LANES]

    put(0, jnp.sum(back_normed * unit, axis=0, keepdims=True))
    put(per, jnp.sum(back_normed, axis=0, keepdims=True))
    at = (2 + 3 * width) * per
    put(at, dot32(jnp.ones((8, rows), BF16), query, (1, 1))[0:1])
    put(at + per, jnp.sum(flat[:, width:].astype(F32), axis=0, keepdims=True))
    lines[at + 2 * per :, :] = jnp.zeros((lines.shape[0] - at - 2 * per, LANES), F32)
    core = info_ref[0] % 2

    def window(step, _):
        for ref, which in ((send_ref, 1 - core), (keep_ref, core)):
            write_window((2 * step + which) * size, lines, ref, step)
        return 0

    lax.fori_loop(0, LATE_CHUNKS // 2, window, 0)


def finish(size, info, x, gain, shift, w_qkv, back_hidden, back):
    rows, width = x.shape
    window = jax.ShapeDtypeStruct((LATE_CHUNKS // 2, LATE_WINDOW, LANES), BF16)
    shapes = [jax.ShapeDtypeStruct((rows, width), BF16), window, window]
    operands = [x, gain, shift, w_qkv, back_hidden, *back]
    scratch = [
        pltpu.VMEM((HEADS, HEAD_DIM, rows), BF16),
        pltpu.VMEM((rows, 2 * width), BF16),
        pltpu.VMEM((-(-(LATE_CHUNKS - 1) * size // 8) * 8 + LATE_WINDOW + 8, LANES), F32),
    ]
    kernel = functools.partial(finish_kernel, size)
    return one_step(kernel, info, operands, shapes, scratch, rows * width)


def along_g(values):
    return lax.all_to_all(values, "g", 0, 0, tiled=True)


def hold(values, after):
    return lax.optimization_barrier((values, list(after)))[0] if len(after) > 0 else values


def exchange(parts):
    return [lax.ppermute(part, ("x", "c"), [(i, i ^ n) for i in range(4)]) for part, n in zip(parts, (2, 1, 3))]


class Plane:
    def gather_keys(self, kv):
        return [kv[None], swap(kv, "f")[None]]

    def gather_queries(self, q):
        return [q] + exchange([q] * 3)

    gather_grads = gather_queries

    def gather_first(self, values):
        over = swap(values, "x")
        return [values, over, swap(values, "c"), swap(over, "c")]

    def gather_parts(self, outs):
        return [outs[0]] + exchange(outs[1:4])

    def gather_back(self, outs):
        kept, sent = outs[4][0], outs[5][0]
        shape = (kept.shape[0], -1, PAIR)
        return kept.reshape(shape), swap(sent, "f").reshape(shape), self.gather_parts(outs)

    def sum_back(self, after, parts):
        return sum_back(after, *parts)


class AnyPlane:
    def __init__(self, clips, times, part):
        self.clips, self.times, self.part = clips, times, part

    def split(self, values):
        groups, rows, width = values.shape
        values = values.reshape(groups, rows, self.clips, self.times, -1).transpose(3, 0, 1, 2, 4)
        return values.reshape(self.times, groups, rows, width // self.times)

    def gather_keys(self, kv):
        return [lax.all_gather(kv, "f")]

    def gather_queries(self, q):
        groups, tiles, rows, lanes = q.shape
        q = lax.all_gather(q.transpose(0, 2, 1, 3).reshape(groups, rows, -1, self.part), "t")
        return [q.transpose(1, 3, 2, 0, 4).reshape(groups, -1, rows, self.times * self.part)]

    def gather_grads(self, values):
        groups, rows, _ = values.shape
        values = lax.all_gather(values.reshape(groups, rows, -1, self.part), "t")
        return [values.transpose(1, 2, 3, 0, 4).reshape(groups, rows, -1)]

    gather_first = gather_grads

    def gather_parts(self, outs):
        return list(lax.all_to_all(self.split(outs[0]), "t", 0, 0, tiled=True))

    def gather_back(self, outs):
        return outs

    def sum_back(self, after, outs):
        back_q = lax.psum_scatter(self.split(outs[0]), "t", scatter_dimension=0, tiled=False)
        back_kv = lax.psum_scatter(outs[1], "f", scatter_dimension=0, tiled=False).reshape(GROUPS, -1, PAIR)
        back_q = back_q.reshape(GROUPS, HEAD_DIM, -1, LANES).transpose(0, 2, 1, 3).reshape(GROUPS, -1, LANES)
        return jnp.concatenate([back_kv, back_q], axis=1)


def layer_norm(values, scaling, offset):
    row_mean = jnp.mean(values, axis=-1, keepdims=True)
    centred = values - row_mean
    spread = jnp.mean(centred * centred, axis=-1, keepdims=True)
    return centred * lax.rsqrt(spread + EPSILON) * scaling + offset


def gelu_exact(values):
    return jax.nn.gelu(values, approximate=False)


def per_device(
    time_axes,
    tokens,
    out_grad,
    lengths,
    norm1_gain,
    norm1_shift,
    w_qkv,
    query_bias,
    value_bias,
    w_proj,
    proj_bias,
    norm2_gain,
    norm2_shift,
    w_fc1,
    fc1_bias,
    w_fc2,
    fc2_bias,
    moment,
    ema_decay,
):
    clips, freq_rows, frames, width = tokens.shape
    part = freq_rows * frames
    rows = clips * part
    times = lax.axis_size(time_axes)
    devices = lax.axis_size("f") * GROUPS * times
    early_index = lax.axis_index(time_axes)
    fast = time_axes == ("x", "c")
    plane = Plane() if fast else AnyPlane(clips, times, part)
    first_frame = (lax.axis_index("g") * times + early_index) * frames
    frame = first_frame + lax.broadcasted_iota(jnp.int32, (1, freq_rows, frames), 2)
    keep_rows = (frame < lengths[:, None, None]).astype(F32).reshape(rows, 1)
    info = jnp.concatenate([early_index.astype(jnp.int32).reshape(1), lengths])

    x = tokens.reshape(rows, width)
    packs = start(x, norm1_gain, norm1_shift, w_qkv, query_bias, value_bias)
    attended, kept = [], []

    def fetch(values, heads, after):
        got = along_g(values)
        pairs, queries = hold((got[:, : heads * rows], got[:, heads * rows :]), after)
        kv = plane.gather_keys(pairs.reshape(GROUPS, heads * clips, part, PAIR))
        return kv, plane.gather_queries(queries.reshape(GROUPS, -1, HEAD_DIM, LANES))

    def merged(after, parts):
        out, low = merge(parts, after)
        kept.append(out)
        attended.append(along_g(hold(low, attended[-1:])))
        return low

    def alone(head):
        return fast and head == GROUP_HEADS - 1

    def run(head, clip, outs, after):
        kv, q = fetched[min(head, 1)]
        place = max(head - 1, 0) * clips + clip
        outs, held = ((), 1) if alone(head) else (outs, clips)
        *outs, token = attend(info, kv, q, place, clip, held, times, frames, outs, after)
        return outs, token

    fetched = [fetch(packs[0], 1, [])]
    fetched.append(fetch(packs[1], GROUP_HEADS - 1, fetched[0][0][1:] + fetched[0][1][1:]))
    parts = None
    for head in range(GROUP_HEADS):
        outs, token = run(head, 0, (), [] if head == 0 else [token])
        after = [token]
        if head > 0:
            after.append(merged(token, parts))
        come = fetched[1][0][1:] + fetched[1][1][1:] if head == 0 else []
        if alone(head):
            half = plane.gather_parts(outs)
            come = half[1:]
        for clip in range(1, clips):
            outs, token = run(head, clip, outs, after)
        parts = plane.gather_parts(hold(outs, come))
    if fast:
        merged(token, half)
    merged(token, parts)
    if fast:
        size = moment.shape[0] // LANES
        block_out, back_hidden, early, grad = middle(
            x, out_grad.reshape(rows, width), keep_rows, w_proj, proj_bias, norm2_gain, norm2_shift, w_fc1, fc1_bias,
            w_fc2, fc2_bias, attended,
        )
        block_out = block_out.reshape(tokens.shape)
        early_windows = pack_early(devices, size, *early)
    else:
        attended_low = jnp.concatenate(attended, axis=1).reshape(width, rows)
        branch = dot32(attended_low, w_proj, (0, 0)) + proj_bias
        hidden = x.astype(F32) + branch
        normed2, norm2_pull = jax.vjp(layer_norm, hidden, norm2_gain, norm2_shift)
        normed2_low = normed2.astype(BF16)
        preactive = dot32(normed2_low, w_fc1, (1, 0)) + fc1_bias
        activated, gelu_pull = jax.vjp(gelu_exact, preactive)
        activated_low = activated.astype(BF16)
        branch2 = dot32(activated_low, w_fc2, (1, 0)) + fc2_bias
        block_out = ((hidden + branch2) * keep_rows).astype(BF16).reshape(tokens.shape)
        grad_out = out_grad.astype(F32).reshape(rows, width) * keep_rows
        back_branch2 = grad_out.astype(BF16)
        grad_fc2_bias = jnp.sum(back_branch2.astype(F32), axis=0)
        back_activated = dot32(back_branch2, w_fc2, (1, 1))
        back_preactive = gelu_pull(back_activated)[0].astype(BF16)
        grad_fc1_bias = jnp.sum(back_preactive.astype(F32), axis=0)
        back_normed2 = dot32(back_preactive, w_fc1, (1, 1))
        back_hidden_norm, grad_norm2_gain, grad_norm2_shift = norm2_pull(back_normed2)
        back_hidden = grad_out + back_hidden_norm
        back_branch = back_hidden.astype(BF16)
        grad_proj_bias = jnp.sum(back_branch.astype(F32), axis=0)
        back_attended = dot32(w_proj, back_branch, (1, 1)).astype(BF16)
        early_windows = info
        grad = back_attended.reshape(GROUPS, -1, rows)
    ready = grad_rows_of(along_g(grad), kept, early_windows)
    back, parts, token = [], None, None
    grads = plane.gather_first(ready[0])
    if fast:
        early_sum = hold(early_windows, grads[:1]).reshape(2, 2, 2, GROUPS, EARLY_WINDOW, LANES)
        early_sum = lax.psum_scatter(early_sum, "c", scatter_dimension=0, tiled=False)

    def run_back(head, clip, outs, after):
        kv, q = fetched[min(head, 1)]
        place = max(head - 1, 0) * clips + clip
        outs, held = ((), 1) if alone(head) else (outs, clips)
        *outs, token = attend_back(info, kv, q, grads, place, clip, held, times, frames, outs, after)
        return outs, token

    for head in range(GROUP_HEADS):
        outs, token = run_back(head, 0, (), [] if head == 0 else [token])
        after = [token]
        if head > 0:
            after += [plane.sum_back(token, parts)] + back
            back.append(along_g(hold(after[1], back)))
        if fast and head == 0:
            early_sum = hold(early_sum, [token])
            after.append(early_sum)
        come = []
        if head + 1 < GROUP_HEADS:
            later = plane.gather_grads(hold(ready[head + 1], after))
            come = later[1:]
        if alone(head):
            half = plane.gather_back(outs)
            come = [half[1]] + half[2][1:]
        for clip in range(1, clips):
            outs, token = run_back(head, clip, outs, after)
        outs = hold(outs, come)
        if fast and head == 0:
            early_sum = hold(early_sum, come + [token]).reshape(4, GROUPS, EARLY_WINDOW, LANES)
            early_sum = lax.psum_scatter(early_sum, ("x", "f"), scatter_dimension=0, tiled=False)
        if head + 1 < GROUP_HEADS:
            grads = later
        parts = plane.gather_back(outs)
    if fast:
        back.append(along_g(hold(plane.sum_back(token, half), back[-1:])))
    back.append(along_g(hold(plane.sum_back(token, parts), back[-1:])))
    if fast:
        input_grad, *late_windows = finish(
            size, info, x, norm1_gain, norm1_shift, w_qkv, back_hidden, back
        )
        input_grad = input_grad.reshape(tokens.shape)
        early_sum = lax.psum_scatter(hold(early_sum, [back[-1]]), "g", scatter_dimension=0, tiled=False).astype(F32)
        late_sum = reduce_late(*late_windows, early_sum)
        weight_grad = own_chunk(lax.optimization_barrier(early_sum), late_sum, moment.shape[0])
    else:
        back = jnp.stack(back, axis=1)
        back_kv = back[:, :, :rows].transpose(2, 0, 1, 3).reshape(rows, 2 * width)
        back_q = back[:, :, rows:].reshape(GROUPS, GROUP_HEADS, -1, HEAD_DIM, LANES).transpose(0, 1, 3, 2, 4).reshape(width, rows)
        grad_query_bias = jnp.sum(back_q.astype(F32), axis=1)
        grad_kv_bias = jnp.sum(back_kv.astype(F32), axis=0)
        grad_value_bias = grad_kv_bias.reshape(HEADS, 2, HEAD_DIM)[:, 1].reshape(width)
        normed, norm1_pull = jax.vjp(layer_norm, x.astype(F32), norm1_gain, norm1_shift)
        normed_low = normed.astype(BF16)
        head_dims = (width, GROUPS, GROUP_HEADS, HEAD_DIM)
        w_q = w_qkv[:, :width]
        w_kv = [w_qkv[:, width : 2 * width].reshape(head_dims), w_qkv[:, 2 * width :].reshape(head_dims)]
        w_kv = jnp.stack(w_kv, axis=3).reshape(width, 2 * width)
        back_normed = dot32(back_q, w_q, (0, 1)) + dot32(back_kv, w_kv, (1, 1))
        back_input_norm, grad_norm1_gain, grad_norm1_shift = norm1_pull(back_normed)
        input_grad = (back_hidden + back_input_norm).astype(BF16).reshape(tokens.shape)
        grad_proj = dot32(attended_low, back_branch, (1, 0))
        grad_fc1 = dot32(normed2_low, back_preactive, (0, 0))
        grad_fc2 = dot32(activated_low, back_branch2, (0, 0))
        grad_q = dot32(normed_low, back_q, (0, 1))
        grad_kv = dot32(normed_low, back_kv, (0, 0)).reshape(width, HEADS, 2, HEAD_DIM)
        grad_qkv = jnp.concatenate([grad_q, grad_kv[:, :, 0].reshape(width, width), grad_kv[:, :, 1].reshape(width, width)], axis=1)
        joined = jnp.concatenate(
            [
                grad_norm1_gain,
                grad_norm1_shift,
                grad_qkv.reshape(-1),
                grad_query_bias,
                grad_value_bias,
                grad_proj.reshape(-1),
                grad_proj_bias,
                grad_norm2_gain,
                grad_norm2_shift,
                grad_fc1.reshape(-1),
                grad_fc1_bias,
                grad_fc2.reshape(-1),
                grad_fc2_bias,
            ]
        ).astype(BF16)
        padding = moment.shape[0] * devices - joined.shape[0]
        joined = jnp.concatenate([joined, jnp.zeros((padding,), BF16)])
        weight_grad = lax.psum_scatter(joined, ("f", "g") + time_axes, scatter_dimension=0, tiled=True).astype(F32)
    new_moment = ema_decay[0] * moment + (1.0 - ema_decay[0]) * weight_grad
    return (block_out, input_grad, weight_grad, new_moment)


def solution(mesh):
    freqs, times = mesh.shape["freq"], mesh.shape["tm"]
    if (freqs, times) == (2, 16):
        time_sizes, time_axes = (2, 2), ("x", "c")
    else:
        time_sizes, time_axes = (times // GROUPS,), ("t",)
    fine = Mesh(mesh.devices.reshape(freqs, GROUPS, *time_sizes), ("f", "g") + time_axes)
    patches = P(None, "f", ("g",) + time_axes, None)
    flat = P(("f", "g") + time_axes)
    return jax.shard_map(
        functools.partial(per_device, time_axes),
        mesh=fine,
        in_specs=(patches, patches) + (P(),) * 14 + (flat, P()),
        out_specs=(patches, patches, flat, flat),
        check_vma=False,
    )
```

profile of v0, /device:TPU:0, one launch (start us, length us, event | category | flops | bytes accessed | tf_op | source)
XLA Modules:
  0.0 554.7 jit_solution(7556546710713432338)
XLA Ops:
  7.2 6.1 %shard_map.201 = (bf16[4,768,128]{2,1,0:T(8,128)(2,1)}, bf16[4,1536,128]{2,1,0:T(8,128)(2,1)}) custom-call(bf16[512,768]{1,0:T(8,128)(2,1)} %bitcast.82, f32[768]{0:T(1024)} %gain_ref.5, f32[768]{0:T(1024)} %shift_ref.5, bf16[768,2304]{1,0:T(8,128)(2,1)} %w_ref.3, f32[768]{0:T(1024)} %query_bias_ref.1, f32[768]{0:T(1024)} %value_bias_ref.1), custom_call_target="tpu_custom_call" | custom-call | flops 1811939328 | bytes 3623878 | tf_op jit(solution)/shard_map/pallas_call | solution.py:494
  13.2 26.4 %all_to_all.60 = bf16[4,768,128]{2,1,0:T(8,128)(2,1)S(1)} all-to-all(bf16[4,768,128]{2,1,0:T(8,128)(2,1)} %get-tuple-element.144), channel_id=1, replica_groups=mesh['f'=2,'g'=4,'x'=2,'c'=2] {'g'}, dimensions={0} | all-to-all | bytes 1572864 | tf_op jit(solution)/shard_map/all_to_all | solution.py:663
  39.7 3.6 all-to-all-start
  47.8 31.5 %all-to-all-done = bf16[4,1536,128]{2,1,0:T(8,128)(2,1)S(1)} async-done(((bf16[4,1536,128]{2,1,0:T(8,128)(2,1)}), bf16[4,1536,128]{2,1,0:T(8,128)(2,1)S(1)}, u32[]{:S(2)}, u32[]{:S(2)}) %all-to-all-start) | async-done | bytes 1572896 | tf_op jit(solution)/shard_map/all_to_all | solution.py:663
  83.9 5.7 %shard_map.202 = (bf16[4,80,512]{2,1,0:T(8,128)(2,1)}, bf16[4,80,512]{2,1,0:T(8,128)(2,1)}, bf16[4,80,512]{2,1,0:T(8,128)(2,1)}, bf16[4,80,512]{2,1,0:T(8,128)(2,1)}, f32[8,128]{1,0:T(8,128)}) custom-call(s32[3]{0:T(128)} %pad_add_fusion.info_ref, bf16[1,4,2,256,128]{4,3,2,1,0:T(8,128)(2,1)} %bitcast.10.refs_0_, ...), custom_call_target="tpu_custom_call" | custom-call | flops 2147483648 | bytes 524288 | tf_op jit(solution)/shard_map/pallas_call | solution.py:142
  89.6 12.5 %shard_map.203 = (bf16[4,80,512]{2,1,0:T(8,128)(2,1)}, bf16[4,80,512]{2,1,0:T(8,128)(2,1)}, bf16[4,80,512]{2,1,0:T(8,128)(2,1)}, bf16[4,80,512]{2,1,0:T(8,128)(2,1)}, f32[8,128]{1,0:T(8,128)}) custom-call(s32[3]{0:T(128)} %pad_add_fusion.info_ref, ...), custom_call_target="tpu_custom_call", output_to_operand_aliasing={{0}: (7, {}), {1}: (8, {}), {2}: (9, {}), {3}: (10, {})} | custom-call | flops 2147483648 | bytes 524288 | tf_op jit(solution)/shard_map/pallas_call | solution.py:142
  106.2 5.9 %shard_map.204 = (bf16[4,80,512]{2,1,0:T(8,128)(2,1)}, bf16[4,80,512]{2,1,0:T(8,128)(2,1)}, bf16[4,80,512]{2,1,0:T(8,128)(2,1)}, bf16[4,80,512]{2,1,0:T(8,128)(2,1)}, f32[8,128]{1,0:T(8,128)}) custom-call(s32[3]{0:T(128)} %pad_add_fusion.info_ref, bf16[1,4,4,256,128]{4,3,2,1,0:T(8,128)(2,1)} %bitcast.74, bf16[1,4,4,256,128]{4,3,2,1,0:T(8,128)(2,1)} %bitcast.113, ...), custom_call_target="tpu_custom_call" | custom-call | flops 2147483648 | bytes 524288 | tf_op jit(solution)/shard_map/pallas_call | solution.py:142
  112.1 2.6 collective-permute-done.8.refs_1_
  114.7 6.9 %collective-permute-done.10.refs_3_ = bf16[4,80,512]{2,1,0:T(8,128)(2,1)S(1)} collective-permute-done((bf16[4,80,512]{2,1,0:T(8,128)(2,1)}, bf16[4,80,512]{2,1,0:T(8,128)(2,1)S(1)}, u32[]{:S(2)}, u32[]{:S(2)}) %collective-permute-start.10) | collective-permute-done | bytes 327712 | tf_op jit(solution)/shard_map/ppermute | solution.py:671
  124.8 3.4 all-to-all-start.2
  128.2 12.5 %shard_map.206 = (bf16[4,80,512]{2,1,0:T(8,128)(2,1)}, bf16[4,80,512]{2,1,0:T(8,128)(2,1)}, bf16[4,80,512]{2,1,0:T(8,128)(2,1)}, bf16[4,80,512]{2,1,0:T(8,128)(2,1)}, f32[8,128]{1,0:T(8,128)}) custom-call(s32[3]{0:T(128)} %pad_add_fusion.info_ref, ...), custom_call_target="tpu_custom_call", output_to_operand_aliasing={{0}: (7, {}), {1}: (8, {}), {2}: (9, {}), {3}: (10, {})} | custom-call | flops 2147483648 | bytes 524288 | tf_op jit(solution)/shard_map/pallas_call | solution.py:142
  142.9 5.7 %shard_map.207 = (bf16[4,80,256]{2,1,0:T(8,128)(2,1)}, bf16[4,80,256]{2,1,0:T(8,128)(2,1)}, bf16[4,80,256]{2,1,0:T(8,128)(2,1)}, bf16[4,80,256]{2,1,0:T(8,128)(2,1)}, f32[8,128]{1,0:T(8,128)}) custom-call(s32[3]{0:T(128)} %pad_add_fusion.info_ref, bf16[1,4,4,256,128]{4,3,2,1,0:T(8,128)(2,1)} %bitcast.76, bf16[1,4,4,256,128]{4,3,2,1,0:T(8,128)(2,1)} %bitcast.115, ...), custom_call_target="tpu_custom_call" | custom-call | flops 2147483648 | bytes 524288 | tf_op jit(solution)/shard_map/pallas_call | solution.py:142
  148.6 2.9 collective-permute-done.11.refs_1_
  151.5 5.4 collective-permute-done.13.refs_3_
  157.6 2.5 shard_map.208
  160.1 4.5 all-to-all-start.3
  166.7 12.5 %shard_map.209 = (bf16[4,80,256]{2,1,0:T(8,128)(2,1)}, bf16[4,80,256]{2,1,0:T(8,128)(2,1)}, bf16[4,80,256]{2,1,0:T(8,128)(2,1)}, bf16[4,80,256]{2,1,0:T(8,128)(2,1)}, f32[8,128]{1,0:T(8,128)}) custom-call(s32[3]{0:T(128)} %pad_add_fusion.info_ref, bf16[1,4,4,256,128]{4,3,2,1,0:T(8,128)(2,1)} %bitcast.77, bf16[1,4,4,256,128]{4,3,2,1,0:T(8,128)(2,1)} %bitcast.116, ...), custom_call_target="tpu_custom_call" | custom-call | flops 2147483648 | bytes 524288 | tf_op jit(solution)/shard_map/pallas_call | solution.py:142
  182.1 5.1 all-to-all-start.4
  189.3 5.1 collective-permute-done.17.refs_1_
  198.6 4.8 all-to-all-start.5
  204.4 5.4 all-to-all-done.5.refs_3_
  210.5 22.6 %shard_map.212 = (bf16[512,768]{1,0:T(8,128)(2,1)}, f32[512,768]{1,0:T(8,128)}, bf16[768,512]{1,0:T(8,128)(2,1)}, bf16[512,768]{1,0:T(8,128)(2,1)}, bf16[512,768...) custom-call(bf16[512,768]{1,0:T(8,128)(2,1)} %bitcast.83, ...), custom_call_target="tpu_custom_call" | custom-call | flops 10871635968 | bytes 21743272 | tf_op jit(solution)/shard_map/pallas_call | solution.py:494
  233.1 3.5 all-to-all-start.6
  236.7 26.5 %shard_map.213.refs_4_ = bf16[32,1744,128]{2,1,0:T(8,128)(2,1)} custom-call(bf16[768,512]{1,0:T(8,128)(2,1)} %get-tuple-element.199.att_ref, bf16[512,768]{1,0:T(8,128)(2,1)} %get-tuple-element.200.branch_ref, bf16[512,768]{1,0:T(8,128)(2,1)} %get-tuple-element.201.normed_ref, bf16[512,3072]{1,0:T(8,128)(2,1)} %get-tuple-element.202.pre_ref, ...), custom_call_target="tpu_custom_call" | custom-call | flops 5445255168 | bytes 21270528 | tf_op jit(solution)/shard_map/pallas_call | solution.py:392
  264.1 2.7 shard_map.214
  268.9 8.5 %collective-permute-done.20.refs_7_ = bf16[4,80,512]{2,1,0:T(8,128)(2,1)S(1)} collective-permute-done((bf16[4,80,512]{2,1,0:T(8,128)(2,1)S(1)}, bf16[4,80,512]{2,1,0:T(8,128)(2,1)S(1)}, u32[]{:S(2)}, u32[]{:S(2)}) %collective-permute-start.20) | collective-permute-done | bytes 327712 | tf_op jit(solution)/shard_map/ppermute | solution.py:408
  280.1 9.3 %shard_map.215 = (bf16[4,64,512]{2,1,0:T(8,128)(2,1)}, bf16[4,64,512]{2,1,0:T(8,128)(2,1)}, bf16[4,64,512]{2,1,0:T(8,128)(2,1)}, bf16[4,64,512]{2,1,0:T(8,128)(2...) custom-call(s32[3]{0:T(128)} %pad_add_fusion.info_ref, ...), custom_call_target="tpu_custom_call" | custom-call | flops 5368709120 | bytes 1048576 | tf_op jit(solution)/shard_map/pallas_call | solution.py:231
  293.0 26.1 %shard_map.216 = (bf16[4,64,512]{2,1,0:T(8,128)(2,1)}, bf16[4,64,512]{2,1,0:T(8,128)(2,1)}, bf16[4,64,512]{2,1,0:T(8,128)(2,1)}, bf16[4,64,512]{2,1,0:T(8,128)(2...) custom-call(s32[3]{0:T(128)} %pad_add_fusion.info_ref, ...), custom_call_target="tpu_custom_call", output_to_operand_aliasing={{0}: (11, {}), {1}: (12, {}), {2}: (13, {}), {3}: (14, {}),... | custom-call | flops 5368709120 | bytes 1048576 | tf_op jit(solution)/shard_map/pallas_call | solution.py:231
  324.4 9.0 %shard_map.217 = (bf16[4,64,512]{2,1,0:T(8,128)(2,1)}, bf16[4,64,512]{2,1,0:T(8,128)(2,1)}, bf16[4,64,512]{2,1,0:T(8,128)(2,1)}, bf16[4,64,512]{2,1,0:T(8,128)(2...) custom-call(s32[3]{0:T(128)} %pad_add_fusion.info_ref, ...), custom_call_target="tpu_custom_call" | custom-call | flops 5368709120 | bytes 1048576 | tf_op jit(solution)/shard_map/pallas_call | solution.py:231
  333.7 10.0 %collective-permute-done.29.refs_3_ = bf16[4,64,512]{2,1,0:T(8,128)(2,1)S(1)} collective-permute-done((bf16[4,64,512]{2,1,0:T(8,128)(2,1)S(1)}, bf16[4,64,512]{2,1,0:T(8,128)(2,1)S(1)}, u32[]{:S(2)}, u32[]{:S(2)}) %collective-permute-start.29) | collective-permute-done | bytes 262176 | tf_op jit(solution)/shard_map/ppermute | solution.py:671
  344.5 2.7 shard_map.218.refs_17_
  347.2 4.6 all-to-all-start.7
  354.1 25.9 %shard_map.219 = (bf16[4,64,512]{2,1,0:T(8,128)(2,1)}, bf16[4,64,512]{2,1,0:T(8,128)(2,1)}, bf16[4,64,512]{2,1,0:T(8,128)(2,1)}, bf16[4,64,512]{2,1,0:T(8,128)(2...) custom-call(s32[3]{0:T(128)} %pad_add_fusion.info_ref, ...), custom_call_target="tpu_custom_call", output_to_operand_aliasing={{0}: (11, {}), {1}: (12, {}), {2}: (13, {}), {3}: (14, {}),... | custom-call | flops 5368709120 | bytes 1048576 | tf_op jit(solution)/shard_map/pallas_call | solution.py:231
  380.0 3.2 collective-permute-done.32.refs_9_
  385.3 9.2 %shard_map.220 = (bf16[4,64,256]{2,1,0:T(8,128)(2,1)}, bf16[4,64,256]{2,1,0:T(8,128)(2,1)}, bf16[4,64,256]{2,1,0:T(8,128)(2,1)}, bf16[4,64,256]{2,1,0:T(8,128)(2...) custom-call(s32[3]{0:T(128)} %pad_add_fusion.info_ref, ...), custom_call_target="tpu_custom_call" | custom-call | flops 5368709120 | bytes 1048576 | tf_op jit(solution)/shard_map/pallas_call | solution.py:231
  394.6 5.5 collective-permute-done.36.refs_3_
  400.9 2.7 shard_map.221.refs_11_
  403.6 4.5 all-to-all-start.8
  410.4 25.9 %shard_map.222 = (bf16[4,64,256]{2,1,0:T(8,128)(2,1)}, bf16[4,64,256]{2,1,0:T(8,128)(2,1)}, bf16[4,64,256]{2,1,0:T(8,128)(2,1)}, bf16[4,64,256]{2,1,0:T(8,128)(2...) custom-call(s32[3]{0:T(128)} %pad_add_fusion.info_ref, ...), custom_call_target="tpu_custom_call" | custom-call | flops 5368709120 | bytes 1048576 | tf_op jit(solution)/shard_map/pallas_call | solution.py:231
  439.3 5.1 all-to-all-start.9
  448.6 3.3 collective-permute-done.42.refs_1_
  456.7 17.5 %all_to_all.61.refs_3_ = bf16[4,384,128]{2,1,0:T(8,128)(2,1)} all-to-all(bf16[4,384,128]{2,1,0:T(8,128)(2,1)} %shard_map.224), channel_id=1, replica_groups=mesh['f'=2,'g'=4,'x'=2,'c'=2] {'g'}, dimensions={0} | all-to-all | bytes 786432 | tf_op jit(solution)/shard_map/all_to_all | solution.py:663
  474.3 13.3 %shard_map.225 = (bf16[512,768]{1,0:T(8,128)(2,1)}, bf16[4,1792,128]{2,1,0:T(8,128)(2,1)}, bf16[4,1792,128]{2,1,0:T(8,128)(2,1)}) custom-call(s32[3]{0:T(128)} %pad_add_fusion.info_ref, bf16[512,768]{1,0:T(8,128)(2,1)} %bitcast.84, f32[768]{0:T(1024)} %gain_ref.5, f32[768]{0:T(1024)} %shift_ref.5, bf16[768,2304]{1,0:T(8,128)(2,1)} %w_ref.3, ...), custom_call_target="tpu_custom_call" | custom-call | flops 393216 | bytes 786 | tf_op jit(solution)/shard_map/pallas_call | solution.py:494
  487.6 4.0 collective-permute-done.45
  495.7 10.9 %collective-permute-done.48 = bf16[2,2,448,128]{3,2,0,1:T(8,128)(2,1)S(1)} collective-permute-done((bf16[2,2,448,128]{3,2,0,1:T(8,128)(2,1)S(1)}, bf16[2,2,448,128]{3,2,0,1:T(8,128)(2,1)S(1)}, u32[]{:S(2)}, u32[]{:S(2)}) %collective-permute-start.48) | collective-permute-done | bytes 458784 | tf_op jit(solution)/shard_map/ppermute | solution.py:408
  508.8 5.0 collective-permute-done.49
  515.3 18.2 %all_to_all.62 = bf16[4,448,128]{2,1,0:T(8,128)(2,1)S(1)} all-to-all(bf16[4,448,128]{2,1,0:T(8,128)(2,1)S(1)} %pad_maximum_fusion), channel_id=1, replica_groups=mesh['f'=2,'g'=4,'x'=2,'c'=2] {'g'}, dimensions={0} | all-to-all | bytes 917504 | tf_op jit(solution)/shard_map/all_to_all | solution.py:663
  539.2 4.9 collective-permute-done.52
  (276 shorter events, 83.9 us)
Async XLA Ops:
  39.7 39.6 %all-to-all-start = ((bf16[4,1536,128]{2,1,0:T(8,128)(2,1)}), bf16[4,1536,128]{2,1,0:T(8,128)(2,1)S(1)}, u32[]{:S(2)}, u32[]{:S(2)}) async-start(bf16[4,1536,128]{2,1,0:T(8,128)(2,1)} %get-tuple-element.143), calls=%async_computation | async-start | bytes 3145728 | tf_op jit(solution)/shard_map/all_to_all | solution.py:663
  44.1 35.4 %collective-permute-start = (bf16[4,2,256,128]{3,2,1,0:T(8,128)(2,1)}, bf16[4,2,256,128]{3,2,1,0:T(8,128)(2,1)}, u32[]{:S(2)}, u32[]{:S(2)}) collective-permute-start(bf16[4,2,256,128]{3,2,1,0:T(8,128)(2,1)} %bitcast.3), channel_id=1, source_target_pairs={{0,16},{16,0},{1,17},{17,1},{2,18},{18,2},{3,19},{19,3},{4,20},{20... | collective-permute-start | bytes 1572872 | tf_op jit(solution)/shard_map/ppermute | solution.py:408
  45.6 33.8 %collective-permute-start.1 = (bf16[4,4,64,128]{3,2,1,0:T(8,128)(2,1)S(1)}, bf16[4,4,64,128]{3,2,1,0:T(8,128)(2,1)}, u32[]{:S(2)}, u32[]{:S(2)}) collective-permute-start(bf16[4,4,64,128]{3,2,1,0:T(8,128)(2,1)S(1)} %bitcast.102), channel_id=1, source_target_pairs={{0,2},{1,3},{2,0},{3,1},{4,6},{5,7},{6,4},{7,5},{8,10},{9,11},{10,... | collective-permute-start | bytes 786440 | tf_op jit(solution)/shard_map/ppermute | solution.py:671
  47.2 32.3 %collective-permute-start.2 = (bf16[4,4,64,128]{3,2,1,0:T(8,128)(2,1)S(1)}, bf16[4,4,64,128]{3,2,1,0:T(8,128)(2,1)}, u32[]{:S(2)}, u32[]{:S(2)}) collective-permute-start(bf16[4,4,64,128]{3,2,1,0:T(8,128)(2,1)S(1)} %bitcast.103), channel_id=1, source_target_pairs={{0,1},{1,0},{2,3},{3,2},{4,5},{5,4},{6,7},{7,6},{8,9},{9,8},{10,11... | collective-permute-start | bytes 786440 | tf_op jit(solution)/shard_map/ppermute | solution.py:671
  47.2 32.3 %collective-permute-start.3 = (bf16[4,4,64,128]{3,2,1,0:T(8,128)(2,1)S(1)}, bf16[4,4,64,128]{3,2,1,0:T(8,128)(2,1)}, u32[]{:S(2)}, u32[]{:S(2)}) collective-permute-start(bf16[4,4,64,128]{3,2,1,0:T(8,128)(2,1)S(1)} %bitcast.104), channel_id=1, source_target_pairs={{0,3},{1,2},{2,1},{3,0},{4,7},{5,6},{6,5},{7,4},{8,11},{9,10},{10,... | collective-permute-start | bytes 786440 | tf_op jit(solution)/shard_map/ppermute | solution.py:671
  79.5 24.4 %collective-permute-start.4 = (bf16[4,4,256,128]{3,2,1,0:T(8,128)(2,1)S(1)}, bf16[4,4,256,128]{3,2,1,0:T(8,128)(2,1)S(1)}, u32[]{:S(2)}, u32[]{:S(2)}) collective-permute-start(bf16[4,4,256,128]{3,2,1,0:T(8,128)(2,1)S(1)} %bitcast.73), channel_id=1, source_target_pairs={{0,16},{16,0},{1,17},{17,1},{2,18},{18,2},{3,19},{19,3},{4,20},{20... | collective-permute-start | bytes 3145736 | tf_op jit(solution)/shard_map/ppermute | solution.py:408
  81.1 21.0 %collective-permute-start.5 = (bf16[4,8,64,128]{3,2,1,0:T(8,128)(2,1)S(1)}, bf16[4,8,64,128]{3,2,1,0:T(8,128)(2,1)}, u32[]{:S(2)}, u32[]{:S(2)}) collective-permute-start(bf16[4,8,64,128]{3,2,1,0:T(8,128)(2,1)S(1)} %bitcast.85), channel_id=1, source_target_pairs={{0,2},{1,3},{2,0},{3,1},{4,6},{5,7},{6,4},{7,5},{8,10},{9,11},{10,... | collective-permute-start | bytes 1572872 | tf_op jit(solution)/shard_map/ppermute | solution.py:671
  82.6 19.5 %collective-permute-start.6 = (bf16[4,8,64,128]{3,2,1,0:T(8,128)(2,1)S(1)}, bf16[4,8,64,128]{3,2,1,0:T(8,128)(2,1)}, u32[]{:S(2)}, u32[]{:S(2)}) collective-permute-start(bf16[4,8,64,128]{3,2,1,0:T(8,128)(2,1)S(1)} %bitcast.86), channel_id=1, source_target_pairs={{0,1},{1,0},{2,3},{3,2},{4,5},{5,4},{6,7},{7,6},{8,9},{9,8},{10,11... | collective-permute-start | bytes 1572872 | tf_op jit(solution)/shard_map/ppermute | solution.py:671
  82.6 21.3 %collective-permute-start.7 = (bf16[4,8,64,128]{3,2,1,0:T(8,128)(2,1)S(1)}, bf16[4,8,64,128]{3,2,1,0:T(8,128)(2,1)}, u32[]{:S(2)}, u32[]{:S(2)}) collective-permute-start(bf16[4,8,64,128]{3,2,1,0:T(8,128)(2,1)S(1)} %bitcast.87), channel_id=1, source_target_pairs={{0,3},{1,2},{2,1},{3,0},{4,7},{5,6},{6,5},{7,4},{8,11},{9,10},{10,... | collective-permute-start | bytes 1572872 | tf_op jit(solution)/shard_map/ppermute | solution.py:671
  103.9 10.8 %collective-permute-start.8 = (bf16[4,80,512]{2,1,0:T(8,128)(2,1)}, bf16[4,80,512]{2,1,0:T(8,128)(2,1)S(1)}, u32[]{:S(2)}, u32[]{:S(2)}) collective-permute-start(bf16[4,80,512]{2,1,0:T(8,128)(2,1)} %get-tuple-element.159), channel_id=1, source_target_pairs={{0,2},{1,3},{2,0},{3,1},{4,6},{5,7},{6,4},{7,5},{8,10},{9,11},{10,... | collective-permute-start | bytes 983048 | tf_op jit(solution)/shard_map/ppermute | solution.py:671
  106.1 15.6 %collective-permute-start.10 = (bf16[4,80,512]{2,1,0:T(8,128)(2,1)}, bf16[4,80,512]{2,1,0:T(8,128)(2,1)S(1)}, u32[]{:S(2)}, u32[]{:S(2)}) collective-permute-start(bf16[4,80,512]{2,1,0:T(8,128)(2,1)} %get-tuple-element.161), channel_id=1, source_target_pairs={{0,3},{1,2},{2,1},{3,0},{4,7},{5,6},{6,5},{7,4},{8,11},{9,10},{10,... | collective-permute-start | bytes 983048 | tf_op jit(solution)/shard_map/ppermute | solution.py:671
  124.8 35.3 %all-to-all-start.2 = ((bf16[4,64,512]{2,1,0:T(8,128)(2,1)}), bf16[4,64,512]{2,1,0:T(8,128)(2,1)S(1)}, u32[]{:S(2)}, u32[]{:S(2)}) async-start(bf16[4,64,512]{2,1,0:T(8,128)(2,1)} %get-tuple-element.162.refs_11_), calls=%async_computation.2 | async-start | bytes 524288 | tf_op jit(solution)/shard_map/all_to_all | solution.py:663
  140.7 10.8 %collective-permute-start.11 = (bf16[4,80,512]{2,1,0:T(8,128)(2,1)}, bf16[4,80,512]{2,1,0:T(8,128)(2,1)S(1)}, u32[]{:S(2)}, u32[]{:S(2)}) collective-permute-start(bf16[4,80,512]{2,1,0:T(8,128)(2,1)} %get-tuple-element.170), channel_id=1, source_target_pairs={{0,2},{1,3},{2,0},{3,1},{4,6},{5,7},{6,4},{7,5},{8,10},{9,11},{10,... | collective-permute-start | bytes 983048 | tf_op jit(solution)/shard_map/ppermute | solution.py:671
  142.1 14.8 %collective-permute-start.13 = (bf16[4,80,512]{2,1,0:T(8,128)(2,1)}, bf16[4,80,512]{2,1,0:T(8,128)(2,1)S(1)}, u32[]{:S(2)}, u32[]{:S(2)}) collective-permute-start(bf16[4,80,512]{2,1,0:T(8,128)(2,1)} %get-tuple-element.172), channel_id=1, source_target_pairs={{0,3},{1,2},{2,1},{3,0},{4,7},{5,6},{6,5},{7,4},{8,11},{9,10},{10,... | collective-permute-start | bytes 983048 | tf_op jit(solution)/shard_map/ppermute | solution.py:671
  160.1 22.0 %all-to-all-start.3 = ((bf16[4,64,512]{2,1,0:T(8,128)(2,1)}), bf16[4,64,512]{2,1,0:T(8,128)(2,1)S(1)}, u32[]{:S(2)}, u32[]{:S(2)}) async-start(bf16[4,64,512]{2,1,0:T(8,128)(2,1)} %get-tuple-element.174.refs_7_), calls=%async_computation.3 | async-start | bytes 524288 | tf_op jit(solution)/shard_map/all_to_all | solution.py:663
  164.6 14.6 %collective-permute-start.14 = (bf16[4,80,256]{2,1,0:T(8,128)(2,1)S(1)}, bf16[4,80,256]{2,1,0:T(8,128)(2,1)S(1)}, u32[]{:S(2)}, u32[]{:S(2)}) collective-permute-start(bf16[4,80,256]{2,1,0:T(8,128)(2,1)S(1)} %copy-done.62), channel_id=1, source_target_pairs={{0,2},{1,3},{2,0},{3,1},{4,6},{5,7},{6,4},{7,5},{8,10},{9,11},{10,... | collective-permute-start | bytes 491528 | tf_op jit(solution)/shard_map/ppermute | solution.py:671
  165.5 13.7 %collective-permute-start.15 = (bf16[4,80,256]{2,1,0:T(8,128)(2,1)S(1)}, bf16[4,80,256]{2,1,0:T(8,128)(2,1)S(1)}, u32[]{:S(2)}, u32[]{:S(2)}) collective-permute-start(bf16[4,80,256]{2,1,0:T(8,128)(2,1)S(1)} %copy-done.61), channel_id=1, source_target_pairs={{0,1},{1,0},{2,3},{3,2},{4,5},{5,4},{6,7},{7,6},{8,9},{9,8},{10,11... | collective-permute-start | bytes 491528 | tf_op jit(solution)/shard_map/ppermute | solution.py:671
  166.1 13.1 %collective-permute-start.16 = (bf16[4,80,256]{2,1,0:T(8,128)(2,1)S(1)}, bf16[4,80,256]{2,1,0:T(8,128)(2,1)S(1)}, u32[]{:S(2)}, u32[]{:S(2)}) collective-permute-start(bf16[4,80,256]{2,1,0:T(8,128)(2,1)S(1)} %copy-done.60), channel_id=1, source_target_pairs={{0,3},{1,2},{2,1},{3,0},{4,7},{5,6},{6,5},{7,4},{8,11},{9,10},{10,... | collective-permute-start | bytes 491528 | tf_op jit(solution)/shard_map/ppermute | solution.py:671
  182.1 16.5 %all-to-all-start.4 = ((bf16[4,64,256]{2,1,0:T(8,128)(2,1)}), bf16[4,64,256]{2,1,0:T(8,128)(2,1)S(1)}, u32[]{:S(2)}, u32[]{:S(2)}) async-start(bf16[4,64,256]{2,1,0:T(8,128)(2,1)} %get-tuple-element.181), calls=%async_computation.4 | async-start | bytes 262144 | tf_op jit(solution)/shard_map/all_to_all | solution.py:663
  198.6 11.3 %all-to-all-start.5 = ((bf16[4,64,256]{2,1,0:T(8,128)(2,1)}), bf16[4,64,256]{2,1,0:T(8,128)(2,1)S(1)}, u32[]{:S(2)}, u32[]{:S(2)}) async-start(bf16[4,64,256]{2,1,0:T(8,128)(2,1)} %get-tuple-element.191), calls=%async_computation.5 | async-start | bytes 262144 | tf_op jit(solution)/shard_map/all_to_all | solution.py:663
  233.1 30.1 %all-to-all-start.6 = ((bf16[4,192,512]{2,1,0:T(8,128)(2,1)}), bf16[4,192,512]{2,1,0:T(8,128)(2,1)S(1)}, u32[]{:S(2)}, u32[]{:S(2)}) async-start(bf16[4,192,512]{2,1,0:T(8,128)(2,1)} %get-tuple-element.194), calls=%async_computation.6 | async-start | bytes 1572864 | tf_op jit(solution)/shard_map/all_to_all | solution.py:663
  236.6 54.3 %reduce-scatter.6.cloned.1.call-start = ((), (), s32[]{:S(2)}) async-start(), calls=%async_computation.15 | async-start | bytes 21430272 | tf_op jit(solution)/shard_map/reduce_scatter | solution.py:863
  266.8 220.8 %reduce-scatter.10.cloned.1.call-start = ((), (), s32[]{:S(2)}) async-start(), calls=%async_computation.17 | async-start | bytes 8929280
  267.7 9.6 %collective-permute-start.20 = (bf16[4,80,512]{2,1,0:T(8,128)(2,1)S(1)}, bf16[4,80,512]{2,1,0:T(8,128)(2,1)S(1)}, u32[]{:S(2)}, u32[]{:S(2)}) collective-permute-start(bf16[4,80,512]{2,1,0:T(8,128)(2,1)S(1)} %copy-done.51), channel_id=1, source_target_pairs={{0,2},{2,0},{1,3},{3,1},{4,6},{6,4},{5,7},{7,5},{8,10},{10,8},{9,1... | collective-permute-start | bytes 983048 | tf_op jit(solution)/shard_map/ppermute | solution.py:408
  290.9 28.2 %collective-permute-start.23 = (bf16[4,80,512]{2,1,0:T(8,128)(2,1)S(1)}, bf16[4,80,512]{2,1,0:T(8,128)(2,1)S(1)}, u32[]{:S(2)}, u32[]{:S(2)}) collective-permute-start(bf16[4,80,512]{2,1,0:T(8,128)(2,1)S(1)} %copy-done.44), channel_id=1, source_target_pairs={{0,2},{1,3},{2,0},{3,1},{4,6},{5,7},{6,4},{7,5},{8,10},{9,11},{10,... | collective-permute-start | bytes 983048 | tf_op jit(solution)/shard_map/ppermute | solution.py:671
  292.7 26.4 %collective-permute-start.24 = (bf16[4,80,512]{2,1,0:T(8,128)(2,1)S(1)}, bf16[4,80,512]{2,1,0:T(8,128)(2,1)S(1)}, u32[]{:S(2)}, u32[]{:S(2)}) collective-permute-start(bf16[4,80,512]{2,1,0:T(8,128)(2,1)S(1)} %copy-done.44), channel_id=1, source_target_pairs={{0,1},{1,0},{2,3},{3,2},{4,5},{5,4},{6,7},{7,6},{8,9},{9,8},{10,11... | collective-permute-start | bytes 983048 | tf_op jit(solution)/shard_map/ppermute | solution.py:671
  292.7 26.4 %collective-permute-start.25 = (bf16[4,80,512]{2,1,0:T(8,128)(2,1)S(1)}, bf16[4,80,512]{2,1,0:T(8,128)(2,1)S(1)}, u32[]{:S(2)}, u32[]{:S(2)}) collective-permute-start(bf16[4,80,512]{2,1,0:T(8,128)(2,1)S(1)} %copy-done.44), channel_id=1, source_target_pairs={{0,3},{1,2},{2,1},{3,0},{4,7},{5,6},{6,5},{7,4},{8,11},{9,10},{10,... | collective-permute-start | bytes 983048 | tf_op jit(solution)/shard_map/ppermute | solution.py:671
  320.5 23.2 %collective-permute-start.26 = (bf16[4,2,256,128]{3,2,1,0:T(8,128)(2,1)S(1)}, bf16[4,2,256,128]{3,2,1,0:T(8,128)(2,1)S(1)}, u32[]{:S(2)}, u32[]{:S(2)}) collective-permute-start(bf16[4,2,256,128]{3,2,1,0:T(8,128)(2,1)S(1)} %bitcast.124), channel_id=1, source_target_pairs={{0,16},{16,0},{1,17},{17,1},{2,18},{18,2},{3,19},{19,3},{4,20},{20... | collective-permute-start | bytes 1572872 | tf_op jit(solution)/shard_map/ppermute | solution.py:408
  322.2 11.4 %collective-permute-start.27 = (bf16[4,64,512]{2,1,0:T(8,128)(2,1)S(1)}, bf16[4,64,512]{2,1,0:T(8,128)(2,1)S(1)}, u32[]{:S(2)}, u32[]{:S(2)}) collective-permute-start(bf16[4,64,512]{2,1,0:T(8,128)(2,1)S(1)} %copy-done.57), channel_id=1, source_target_pairs={{0,2},{1,3},{2,0},{3,1},{4,6},{5,7},{6,4},{7,5},{8,10},{9,11},{10,... | collective-permute-start | bytes 786440 | tf_op jit(solution)/shard_map/ppermute | solution.py:671
  323.7 10.0 %collective-permute-start.28 = (bf16[4,64,512]{2,1,0:T(8,128)(2,1)S(1)}, bf16[4,64,512]{2,1,0:T(8,128)(2,1)S(1)}, u32[]{:S(2)}, u32[]{:S(2)}) collective-permute-start(bf16[4,64,512]{2,1,0:T(8,128)(2,1)S(1)} %copy-done.58), channel_id=1, source_target_pairs={{0,1},{1,0},{2,3},{3,2},{4,5},{5,4},{6,7},{7,6},{8,9},{9,8},{10,11... | collective-permute-start | bytes 786440 | tf_op jit(solution)/shard_map/ppermute | solution.py:671
  323.7 20.0 %collective-permute-start.29 = (bf16[4,64,512]{2,1,0:T(8,128)(2,1)S(1)}, bf16[4,64,512]{2,1,0:T(8,128)(2,1)S(1)}, u32[]{:S(2)}, u32[]{:S(2)}) collective-permute-start(bf16[4,64,512]{2,1,0:T(8,128)(2,1)S(1)} %copy-done.59), channel_id=1, source_target_pairs={{0,3},{1,2},{2,1},{3,0},{4,7},{5,6},{6,5},{7,4},{8,11},{9,10},{10,... | collective-permute-start | bytes 786440 | tf_op jit(solution)/shard_map/ppermute | solution.py:671
  347.2 56.4 %all-to-all-start.7 = ((bf16[4,768,128]{2,1,0:T(8,128)(2,1)}), bf16[4,768,128]{2,1,0:T(8,128)(2,1)S(1)}, u32[]{:S(2)}, u32[]{:S(2)}) async-start(bf16[4,768,128]{2,1,0:T(8,128)(2,1)} %shard_map.218.refs_17_), calls=%async_computation.8 | async-start | bytes 1572864 | tf_op jit(solution)/shard_map/all_to_all | solution.py:663
  351.8 28.2 %collective-permute-start.30 = (bf16[4,80,512]{2,1,0:T(8,128)(2,1)S(1)}, bf16[4,80,512]{2,1,0:T(8,128)(2,1)S(1)}, u32[]{:S(2)}, u32[]{:S(2)}) collective-permute-start(bf16[4,80,512]{2,1,0:T(8,128)(2,1)S(1)} %copy-done.43), channel_id=1, source_target_pairs={{0,2},{1,3},{2,0},{3,1},{4,6},{5,7},{6,4},{7,5},{8,10},{9,11},{10,... | collective-permute-start | bytes 983048 | tf_op jit(solution)/shard_map/ppermute | solution.py:671
  351.8 28.2 %collective-permute-start.31 = (bf16[4,80,512]{2,1,0:T(8,128)(2,1)S(1)}, bf16[4,80,512]{2,1,0:T(8,128)(2,1)S(1)}, u32[]{:S(2)}, u32[]{:S(2)}) collective-permute-start(bf16[4,80,512]{2,1,0:T(8,128)(2,1)S(1)} %copy-done.43), channel_id=1, source_target_pairs={{0,1},{1,0},{2,3},{3,2},{4,5},{5,4},{6,7},{7,6},{8,9},{9,8},{10,11... | collective-permute-start | bytes 983048 | tf_op jit(solution)/shard_map/ppermute | solution.py:671
  354.1 29.1 %collective-permute-start.32 = (bf16[4,80,512]{2,1,0:T(8,128)(2,1)S(1)}, bf16[4,80,512]{2,1,0:T(8,128)(2,1)S(1)}, u32[]{:S(2)}, u32[]{:S(2)}) collective-permute-start(bf16[4,80,512]{2,1,0:T(8,128)(2,1)S(1)} %copy-done.43), channel_id=1, source_target_pairs={{0,3},{1,2},{2,1},{3,0},{4,7},{5,6},{6,5},{7,4},{8,11},{9,10},{10,... | collective-permute-start | bytes 983048 | tf_op jit(solution)/shard_map/ppermute | solution.py:671
  383.2 16.9 %collective-permute-start.33 = (bf16[4,2,256,128]{3,2,1,0:T(8,128)(2,1)}, bf16[4,2,256,128]{3,2,1,0:T(8,128)(2,1)S(1)}, u32[]{:S(2)}, u32[]{:S(2)}) collective-permute-start(bf16[4,2,256,128]{3,2,1,0:T(8,128)(2,1)} %bitcast.123), channel_id=1, source_target_pairs={{0,16},{16,0},{1,17},{17,1},{2,18},{18,2},{3,19},{19,3},{4,20},{20... | collective-permute-start | bytes 1572872 | tf_op jit(solution)/shard_map/ppermute | solution.py:408
  383.2 11.3 %collective-permute-start.34 = (bf16[4,64,512]{2,1,0:T(8,128)(2,1)}, bf16[4,64,512]{2,1,0:T(8,128)(2,1)S(1)}, u32[]{:S(2)}, u32[]{:S(2)}) collective-permute-start(bf16[4,64,512]{2,1,0:T(8,128)(2,1)} %get-tuple-element.251), channel_id=1, source_target_pairs={{0,2},{1,3},{2,0},{3,1},{4,6},{5,7},{6,4},{7,5},{8,10},{9,11},{10,... | collective-permute-start | bytes 786440 | tf_op jit(solution)/shard_map/ppermute | solution.py:671
  384.5 10.0 %collective-permute-start.35 = (bf16[4,64,512]{2,1,0:T(8,128)(2,1)}, bf16[4,64,512]{2,1,0:T(8,128)(2,1)S(1)}, u32[]{:S(2)}, u32[]{:S(2)}) collective-permute-start(bf16[4,64,512]{2,1,0:T(8,128)(2,1)} %get-tuple-element.252), channel_id=1, source_target_pairs={{0,1},{1,0},{2,3},{3,2},{4,5},{5,4},{6,7},{7,6},{8,9},{9,8},{10,11... | collective-permute-start | bytes 786440 | tf_op jit(solution)/shard_map/ppermute | solution.py:671
  384.5 15.5 %collective-permute-start.36 = (bf16[4,64,512]{2,1,0:T(8,128)(2,1)}, bf16[4,64,512]{2,1,0:T(8,128)(2,1)S(1)}, u32[]{:S(2)}, u32[]{:S(2)}) collective-permute-start(bf16[4,64,512]{2,1,0:T(8,128)(2,1)} %get-tuple-element.253), channel_id=1, source_target_pairs={{0,3},{1,2},{2,1},{3,0},{4,7},{5,6},{6,5},{7,4},{8,11},{9,10},{10,... | collective-permute-start | bytes 786440 | tf_op jit(solution)/shard_map/ppermute | solution.py:671
  403.6 35.7 %all-to-all-start.8 = ((bf16[4,768,128]{2,1,0:T(8,128)(2,1)}), bf16[4,768,128]{2,1,0:T(8,128)(2,1)S(1)}, u32[]{:S(2)}, u32[]{:S(2)}) async-start(bf16[4,768,128]{2,1,0:T(8,128)(2,1)} %shard_map.221.refs_11_), calls=%async_computation.9 | async-start | bytes 1572864 | tf_op jit(solution)/shard_map/all_to_all | solution.py:663
  408.1 28.2 %collective-permute-start.37 = (bf16[4,1,256,128]{3,2,0,1:T(8,128)(2,1)S(1)}, bf16[4,1,256,128]{3,2,0,1:T(8,128)(2,1)S(1)}, u32[]{:S(2)}, u32[]{:S(2)}) collective-permute-start(bf16[4,1,256,128]{3,2,0,1:T(8,128)(2,1)S(1)} %bitcast.125), channel_id=1, source_target_pairs={{0,16},{16,0},{1,17},{17,1},{2,18},{18,2},{3,19},{19,3},{4,20},{20... | collective-permute-start | bytes 786440 | tf_op jit(solution)/shard_map/ppermute | solution.py:408
  408.2 28.2 %collective-permute-start.38 = (bf16[4,64,256]{2,1,0:T(8,128)(2,1)S(1)}, bf16[4,64,256]{2,1,0:T(8,128)(2,1)S(1)}, u32[]{:S(2)}, u32[]{:S(2)}) collective-permute-start(bf16[4,64,256]{2,1,0:T(8,128)(2,1)S(1)} %copy-done.66), channel_id=1, source_target_pairs={{0,2},{1,3},{2,0},{3,1},{4,6},{5,7},{6,4},{7,5},{8,10},{9,11},{10,... | collective-permute-start | bytes 393224 | tf_op jit(solution)/shard_map/ppermute | solution.py:671
  409.8 26.6 %collective-permute-start.39 = (bf16[4,64,256]{2,1,0:T(8,128)(2,1)S(1)}, bf16[4,64,256]{2,1,0:T(8,128)(2,1)S(1)}, u32[]{:S(2)}, u32[]{:S(2)}) collective-permute-start(bf16[4,64,256]{2,1,0:T(8,128)(2,1)S(1)} %copy-done.64), channel_id=1, source_target_pairs={{0,1},{1,0},{2,3},{3,2},{4,5},{5,4},{6,7},{7,6},{8,9},{9,8},{10,11... | collective-permute-start | bytes 393224 | tf_op jit(solution)/shard_map/ppermute | solution.py:671
  410.3 26.1 %collective-permute-start.40 = (bf16[4,64,256]{2,1,0:T(8,128)(2,1)S(1)}, bf16[4,64,256]{2,1,0:T(8,128)(2,1)S(1)}, u32[]{:S(2)}, u32[]{:S(2)}) collective-permute-start(bf16[4,64,256]{2,1,0:T(8,128)(2,1)S(1)} %copy-done.63), channel_id=1, source_target_pairs={{0,3},{1,2},{2,1},{3,0},{4,7},{5,6},{6,5},{7,4},{8,11},{9,10},{10,... | collective-permute-start | bytes 393224 | tf_op jit(solution)/shard_map/ppermute | solution.py:671
  439.3 17.4 %all-to-all-start.9 = ((bf16[4,384,128]{2,1,0:T(8,128)(2,1)}), bf16[4,384,128]{2,1,0:T(8,128)(2,1)S(1)}, u32[]{:S(2)}, u32[]{:S(2)}) async-start(bf16[4,384,128]{2,1,0:T(8,128)(2,1)} %shard_map.223), calls=%async_computation.10 | async-start | bytes 786432 | tf_op jit(solution)/shard_map/all_to_all | solution.py:663
  444.4 89.2 %reduce-scatter.8.cloned.1.call-start = ((), (), s32[]{:S(2)}) async-start(), calls=%async_computation.16 | async-start | bytes 2232320 | tf_op jit(solution)/shard_map/reduce_scatter | solution.py:905
  493.9 12.7 %collective-permute-start.48 = (bf16[2,2,448,128]{3,2,0,1:T(8,128)(2,1)S(1)}, bf16[2,2,448,128]{3,2,0,1:T(8,128)(2,1)S(1)}, u32[]{:S(2)}, u32[]{:S(2)}) collective-permute-start(bf16[2,2,448,128]{3,2,0,1:T(8,128)(2,1)S(1)} %bitcast.100), channel_id=1, source_target_pairs={{0,16},{16,0},{1,17},{17,1},{2,18},{18,2},{3,19},{19,3},{4,20},{20... | collective-permute-start | bytes 1376264 | tf_op jit(solution)/shard_map/ppermute | solution.py:408
  494.1 14.2 %collective-permute-start.46 = (bf16[2,2,448,128]{3,2,0,1:T(8,128)(2,1)S(1)}, bf16[2,2,448,128]{3,2,0,1:T(8,128)(2,1)S(1)}, u32[]{:S(2)}, u32[]{:S(2)}) collective-permute-start(bf16[2,2,448,128]{3,2,0,1:T(8,128)(2,1)S(1)} %bitcast.101), channel_id=1, source_target_pairs={{0,2},{2,0},{1,3},{3,1},{4,6},{6,4},{5,7},{7,5},{8,10},{10,8},{9,1... | collective-permute-start | bytes 1376264 | tf_op jit(solution)/shard_map/ppermute | solution.py:408
  (86 other events, 635.1 us)
Sparse Core Ops, SparseCore 0:
  266.9 23.9 reduce-scatter.5
  319.3 106.5 reduce-scatter.9
  487.7 38.7 reduce-scatter.7
where the time goes:
time: 562 us; the launch traced here: 555 us
  Pallas kernels  250 us (44%)
  waiting for transfers between devices  128 us (23%)
  starting transfers between devices  80.7 us (14%)
  blocking collectives  62.1 us (11%)
  between operations  15.5 us (3%)
  local copies, waits for them, and re-layouts  13 us (2%)
  other arithmetic  5.73 us (1%)
    pallas_call x6, Pallas kernels, attend_back(): pl.pallas_call(functools.partial(attend_back_kernel, clip, times, frames,...  105 us
    all_to_all x3, blocking collectives, along_g(): return lax.all_to_all(values, 'g', 0, 0, tiled=True)  62.1 us
    pallas_call x6, Pallas kernels, attend(): pl.pallas_call(functools.partial(attend_kernel, clip, times, frames, len(...  54.7 us
    ppermute x36, waiting for transfers between devices, exchange(): lax.ppermute(part, ('x', 'c'), [(i, i ^ n) for i in range(4)])  50.4 us
    pallas_call x3, Pallas kernels, one_step(): pl.pallas_call(kernel, grid_spec=pltpu.PrefetchScalarGridSpec(num_scalar_...  42 us
    all_to_all x9, starting transfers between devices, along_g(): return lax.all_to_all(values, 'g', 0, 0, tiled=True)  39.1 us
    all_to_all x9, waiting for transfers between devices, along_g(): return lax.all_to_all(values, 'g', 0, 0, tiled=True)  36.9 us
    ppermute x14, waiting for transfers between devices, swap(): return lax.ppermute(values, axis, SWAP)  31.7 us
  transfers between devices with their start and end apart: 65, of which 25 were waited for; matrix products, arithmetic and copies ran while one was open for 1% of the time, Pallas kernels for 39%

commit v1 on v0

--- a/solution.py
+++ b/solution.py
@@ -346,7 +346,7 @@
             ref[at] = lines[pl.ds(base, rows + 8), :][s : s + rows].astype(BF16)
 
 
-def pack_early_kernel(size, first, att_ref, branch_ref, normed_ref, pre_ref, act_ref, out_ref, vec_ref, window_ref, lines):
+def pack_early_kernel(size, att_ref, branch_ref, normed_ref, pre_ref, act_ref, out_ref, vec_ref, window_ref, lines):
     step = pl.program_id(0)
 
     @pl.when(step == 0)
@@ -371,13 +371,7 @@
         lines[at : at + per, :] = vec_ref[(3 + blocks) * per :]
         lines[at + per :, :] = jnp.zeros((lines.shape[0] - at - per, LANES), F32)
 
-    @pl.when(step < first)
-    def _():
-        window_ref[...] = jnp.zeros_like(window_ref)
-
-    @pl.when(step >= first)
-    def _():
-        write_window((step - first) * size, lines, window_ref)
+    write_window(step * size, lines, window_ref)
 
 
 def early_order(chunk):
@@ -390,10 +384,10 @@
     whole = [pl.BlockSpec(a.shape, lambda j: (0, 0)) for a in operands]
     entries = chunks * size * LANES
     return pl.pallas_call(
-        functools.partial(pack_early_kernel, size, LATE_CHUNKS),
-        grid=(devices,),
+        functools.partial(pack_early_kernel, size),
+        grid=(chunks,),
         in_specs=whole,
-        out_specs=pl.BlockSpec((1, EARLY_WINDOW, LANES), lambda j: (early_order(j), 0, 0)),
+        out_specs=pl.BlockSpec((1, EARLY_WINDOW, LANES), lambda j: (early_order(j + LATE_CHUNKS), 0, 0)),
         scratch_shapes=[pltpu.VMEM((-(-(chunks - 1) * size // 8) * 8 + EARLY_WINDOW + 8, LANES), F32)],
         out_shape=jax.ShapeDtypeStruct((devices, EARLY_WINDOW, LANES), BF16),
         compiler_params=pltpu.CompilerParams(vmem_limit_bytes=VMEM_LIMIT),

time: 562 us -> 559 us (level)
  no operation moved by 1% of the time
where the time goes in v1:
time: 559 us; the launch traced here: 551 us
  Pallas kernels  247 us (44%)
  waiting for transfers between devices  128 us (23%)
  starting transfers between devices  80.7 us (14%)
  blocking collectives  62.2 us (11%)
  between operations  15.5 us (3%)
  local copies, waits for them, and re-layouts  13 us (2%)
  other arithmetic  5.73 us (1%)
    pallas_call x6, Pallas kernels, attend_back(): pl.pallas_call(functools.partial(attend_back_kernel, clip, times, frames,...  105 us
    all_to_all x3, blocking collectives, along_g(): return lax.all_to_all(values, 'g', 0, 0, tiled=True)  62.2 us
    pallas_call x6, Pallas kernels, attend(): pl.pallas_call(functools.partial(attend_kernel, clip, times, frames, len(...  54.7 us
    ppermute x36, waiting for transfers between devices, exchange(): lax.ppermute(part, ('x', 'c'), [(i, i ^ n) for i in range(4)])  50.4 us
    pallas_call x3, Pallas kernels, one_step(): pl.pallas_call(kernel, grid_spec=pltpu.PrefetchScalarGridSpec(num_scalar_...  42 us
    all_to_all x9, starting transfers between devices, along_g(): return lax.all_to_all(values, 'g', 0, 0, tiled=True)  39 us
    all_to_all x9, waiting for transfers between devices, along_g(): return lax.all_to_all(values, 'g', 0, 0, tiled=True)  36.9 us
    ppermute x14, waiting for transfers between devices, swap(): return lax.ppermute(values, axis, SWAP)  31.6 us
  transfers between devices with their start and end apart: 65, of which 25 were waited for; matrix products, arithmetic and copies ran while one was open for 1% of the time, Pallas kernels for 39%

profile of v1, /device:TPU:0, one launch (start us, length us, event | category | flops | bytes accessed | tf_op | source)
XLA Modules:
  0.0 551.3 jit_solution(11266365587117549657)
XLA Ops:
  7.2 6.1 %shard_map.201 = (bf16[4,768,128]{2,1,0:T(8,128)(2,1)}, bf16[4,1536,128]{2,1,0:T(8,128)(2,1)}) custom-call(bf16[512,768]{1,0:T(8,128)(2,1)} %bitcast.82, f32[768]{0:T(1024)} %gain_ref.5, f32[768]{0:T(1024)} %shift_ref.5, bf16[768,2304]{1,0:T(8,128)(2,1)} %w_ref.3, f32[768]{0:T(1024)} %query_bias_ref.1, f32[768]{0:T(1024)} %value_bias_ref.1), custom_call_target="tpu_custom_call" | custom-call | flops 1811939328 | bytes 3623878 | tf_op jit(solution)/shard_map/pallas_call | solution.py:488
  13.2 26.4 %all_to_all.60 = bf16[4,768,128]{2,1,0:T(8,128)(2,1)S(1)} all-to-all(bf16[4,768,128]{2,1,0:T(8,128)(2,1)} %get-tuple-element.144), channel_id=1, replica_groups=mesh['f'=2,'g'=4,'x'=2,'c'=2] {'g'}, dimensions={0} | all-to-all | bytes 1572864 | tf_op jit(solution)/shard_map/all_to_all | solution.py:657
  39.7 3.6 all-to-all-start
  47.8 31.5 %all-to-all-done = bf16[4,1536,128]{2,1,0:T(8,128)(2,1)S(1)} async-done(((bf16[4,1536,128]{2,1,0:T(8,128)(2,1)}), bf16[4,1536,128]{2,1,0:T(8,128)(2,1)S(1)}, u32[]{:S(2)}, u32[]{:S(2)}) %all-to-all-start) | async-done | bytes 1572896 | tf_op jit(solution)/shard_map/all_to_all | solution.py:657
  83.9 5.7 %shard_map.202 = (bf16[4,80,512]{2,1,0:T(8,128)(2,1)}, bf16[4,80,512]{2,1,0:T(8,128)(2,1)}, bf16[4,80,512]{2,1,0:T(8,128)(2,1)}, bf16[4,80,512]{2,1,0:T(8,128)(2,1)}, f32[8,128]{1,0:T(8,128)}) custom-call(s32[3]{0:T(128)} %pad_add_fusion.info_ref, bf16[1,4,2,256,128]{4,3,2,1,0:T(8,128)(2,1)} %bitcast.10.refs_0_, ...), custom_call_target="tpu_custom_call" | custom-call | flops 2147483648 | bytes 524288 | tf_op jit(solution)/shard_map/pallas_call | solution.py:142
  89.6 12.5 %shard_map.203 = (bf16[4,80,512]{2,1,0:T(8,128)(2,1)}, bf16[4,80,512]{2,1,0:T(8,128)(2,1)}, bf16[4,80,512]{2,1,0:T(8,128)(2,1)}, bf16[4,80,512]{2,1,0:T(8,128)(2,1)}, f32[8,128]{1,0:T(8,128)}) custom-call(s32[3]{0:T(128)} %pad_add_fusion.info_ref, ...), custom_call_target="tpu_custom_call", output_to_operand_aliasing={{0}: (7, {}), {1}: (8, {}), {2}: (9, {}), {3}: (10, {})} | custom-call | flops 2147483648 | bytes 524288 | tf_op jit(solution)/shard_map/pallas_call | solution.py:142
  106.2 5.9 %shard_map.204 = (bf16[4,80,512]{2,1,0:T(8,128)(2,1)}, bf16[4,80,512]{2,1,0:T(8,128)(2,1)}, bf16[4,80,512]{2,1,0:T(8,128)(2,1)}, bf16[4,80,512]{2,1,0:T(8,128)(2,1)}, f32[8,128]{1,0:T(8,128)}) custom-call(s32[3]{0:T(128)} %pad_add_fusion.info_ref, bf16[1,4,4,256,128]{4,3,2,1,0:T(8,128)(2,1)} %bitcast.74, bf16[1,4,4,256,128]{4,3,2,1,0:T(8,128)(2,1)} %bitcast.113, ...), custom_call_target="tpu_custom_call" | custom-call | flops 2147483648 | bytes 524288 | tf_op jit(solution)/shard_map/pallas_call | solution.py:142
  112.1 2.6 collective-permute-done.8.refs_1_
  114.7 6.9 %collective-permute-done.10.refs_3_ = bf16[4,80,512]{2,1,0:T(8,128)(2,1)S(1)} collective-permute-done((bf16[4,80,512]{2,1,0:T(8,128)(2,1)}, bf16[4,80,512]{2,1,0:T(8,128)(2,1)S(1)}, u32[]{:S(2)}, u32[]{:S(2)}) %collective-permute-start.10) | collective-permute-done | bytes 327712 | tf_op jit(solution)/shard_map/ppermute | solution.py:665
  124.8 3.4 all-to-all-start.2
  128.2 12.5 %shard_map.206 = (bf16[4,80,512]{2,1,0:T(8,128)(2,1)}, bf16[4,80,512]{2,1,0:T(8,128)(2,1)}, bf16[4,80,512]{2,1,0:T(8,128)(2,1)}, bf16[4,80,512]{2,1,0:T(8,128)(2,1)}, f32[8,128]{1,0:T(8,128)}) custom-call(s32[3]{0:T(128)} %pad_add_fusion.info_ref, ...), custom_call_target="tpu_custom_call", output_to_operand_aliasing={{0}: (7, {}), {1}: (8, {}), {2}: (9, {}), {3}: (10, {})} | custom-call | flops 2147483648 | bytes 524288 | tf_op jit(solution)/shard_map/pallas_call | solution.py:142
  142.9 5.7 %shard_map.207 = (bf16[4,80,256]{2,1,0:T(8,128)(2,1)}, bf16[4,80,256]{2,1,0:T(8,128)(2,1)}, bf16[4,80,256]{2,1,0:T(8,128)(2,1)}, bf16[4,80,256]{2,1,0:T(8,128)(2,1)}, f32[8,128]{1,0:T(8,128)}) custom-call(s32[3]{0:T(128)} %pad_add_fusion.info_ref, bf16[1,4,4,256,128]{4,3,2,1,0:T(8,128)(2,1)} %bitcast.76, bf16[1,4,4,256,128]{4,3,2,1,0:T(8,128)(2,1)} %bitcast.115, ...), custom_call_target="tpu_custom_call" | custom-call | flops 2147483648 | bytes 524288 | tf_op jit(solution)/shard_map/pallas_call | solution.py:142
  148.6 2.9 collective-permute-done.11.refs_1_
  151.5 5.4 collective-permute-done.13.refs_3_
  157.6 2.5 shard_map.208
  160.1 4.5 all-to-all-start.3
  166.7 12.5 %shard_map.209 = (bf16[4,80,256]{2,1,0:T(8,128)(2,1)}, bf16[4,80,256]{2,1,0:T(8,128)(2,1)}, bf16[4,80,256]{2,1,0:T(8,128)(2,1)}, bf16[4,80,256]{2,1,0:T(8,128)(2,1)}, f32[8,128]{1,0:T(8,128)}) custom-call(s32[3]{0:T(128)} %pad_add_fusion.info_ref, bf16[1,4,4,256,128]{4,3,2,1,0:T(8,128)(2,1)} %bitcast.77, bf16[1,4,4,256,128]{4,3,2,1,0:T(8,128)(2,1)} %bitcast.116, ...), custom_call_target="tpu_custom_call" | custom-call | flops 2147483648 | bytes 524288 | tf_op jit(solution)/shard_map/pallas_call | solution.py:142
  182.1 5.1 all-to-all-start.4
  189.3 5.1 collective-permute-done.17.refs_1_
  198.6 4.8 all-to-all-start.5
  204.4 5.4 all-to-all-done.5.refs_3_
  210.5 22.6 %shard_map.212 = (bf16[512,768]{1,0:T(8,128)(2,1)}, f32[512,768]{1,0:T(8,128)}, bf16[768,512]{1,0:T(8,128)(2,1)}, bf16[512,768]{1,0:T(8,128)(2,1)}, bf16[512,768...) custom-call(bf16[512,768]{1,0:T(8,128)(2,1)} %bitcast.83, ...), custom_call_target="tpu_custom_call" | custom-call | flops 10871635968 | bytes 21743272 | tf_op jit(solution)/shard_map/pallas_call | solution.py:488
  233.1 3.5 all-to-all-start.6
  236.7 23.1 %shard_map.213.refs_4_ = bf16[32,1744,128]{2,1,0:T(8,128)(2,1)} custom-call(bf16[768,512]{1,0:T(8,128)(2,1)} %get-tuple-element.199.att_ref, bf16[512,768]{1,0:T(8,128)(2,1)} %get-tuple-element.200.branch_ref, bf16[512,768]{1,0:T(8,128)(2,1)} %get-tuple-element.201.normed_ref, bf16[512,3072]{1,0:T(8,128)(2,1)} %get-tuple-element.202.pre_ref, ...), custom_call_target="tpu_custom_call" | custom-call | flops 5445255168 | bytes 21270528 | tf_op jit(solution)/shard_map/pallas_call | solution.py:386
  260.6 2.7 shard_map.214
  265.4 8.5 %collective-permute-done.20.refs_7_ = bf16[4,80,512]{2,1,0:T(8,128)(2,1)S(1)} collective-permute-done((bf16[4,80,512]{2,1,0:T(8,128)(2,1)S(1)}, bf16[4,80,512]{2,1,0:T(8,128)(2,1)S(1)}, u32[]{:S(2)}, u32[]{:S(2)}) %collective-permute-start.20) | collective-permute-done | bytes 327712 | tf_op jit(solution)/shard_map/ppermute | solution.py:402
  276.7 9.3 %shard_map.215 = (bf16[4,64,512]{2,1,0:T(8,128)(2,1)}, bf16[4,64,512]{2,1,0:T(8,128)(2,1)}, bf16[4,64,512]{2,1,0:T(8,128)(2,1)}, bf16[4,64,512]{2,1,0:T(8,128)(2...) custom-call(s32[3]{0:T(128)} %pad_add_fusion.info_ref, ...), custom_call_target="tpu_custom_call" | custom-call | flops 5368709120 | bytes 1048576 | tf_op jit(solution)/shard_map/pallas_call | solution.py:231
  289.6 26.1 %shard_map.216 = (bf16[4,64,512]{2,1,0:T(8,128)(2,1)}, bf16[4,64,512]{2,1,0:T(8,128)(2,1)}, bf16[4,64,512]{2,1,0:T(8,128)(2,1)}, bf16[4,64,512]{2,1,0:T(8,128)(2...) custom-call(s32[3]{0:T(128)} %pad_add_fusion.info_ref, ...), custom_call_target="tpu_custom_call", output_to_operand_aliasing={{0}: (11, {}), {1}: (12, {}), {2}: (13, {}), {3}: (14, {}),... | custom-call | flops 5368709120 | bytes 1048576 | tf_op jit(solution)/shard_map/pallas_call | solution.py:231
  321.0 9.0 %shard_map.217 = (bf16[4,64,512]{2,1,0:T(8,128)(2,1)}, bf16[4,64,512]{2,1,0:T(8,128)(2,1)}, bf16[4,64,512]{2,1,0:T(8,128)(2,1)}, bf16[4,64,512]{2,1,0:T(8,128)(2...) custom-call(s32[3]{0:T(128)} %pad_add_fusion.info_ref, ...), custom_call_target="tpu_custom_call" | custom-call | flops 5368709120 | bytes 1048576 | tf_op jit(solution)/shard_map/pallas_call | solution.py:231
  330.3 10.0 %collective-permute-done.29.refs_3_ = bf16[4,64,512]{2,1,0:T(8,128)(2,1)S(1)} collective-permute-done((bf16[4,64,512]{2,1,0:T(8,128)(2,1)S(1)}, bf16[4,64,512]{2,1,0:T(8,128)(2,1)S(1)}, u32[]{:S(2)}, u32[]{:S(2)}) %collective-permute-start.29) | collective-permute-done | bytes 262176 | tf_op jit(solution)/shard_map/ppermute | solution.py:665
  341.1 2.7 shard_map.218.refs_17_
  343.8 4.6 all-to-all-start.7
  350.7 25.9 %shard_map.219 = (bf16[4,64,512]{2,1,0:T(8,128)(2,1)}, bf16[4,64,512]{2,1,0:T(8,128)(2,1)}, bf16[4,64,512]{2,1,0:T(8,128)(2,1)}, bf16[4,64,512]{2,1,0:T(8,128)(2...) custom-call(s32[3]{0:T(128)} %pad_add_fusion.info_ref, ...), custom_call_target="tpu_custom_call", output_to_operand_aliasing={{0}: (11, {}), {1}: (12, {}), {2}: (13, {}), {3}: (14, {}),... | custom-call | flops 5368709120 | bytes 1048576 | tf_op jit(solution)/shard_map/pallas_call | solution.py:231
  376.6 3.2 collective-permute-done.32.refs_9_
  381.9 9.2 %shard_map.220 = (bf16[4,64,256]{2,1,0:T(8,128)(2,1)}, bf16[4,64,256]{2,1,0:T(8,128)(2,1)}, bf16[4,64,256]{2,1,0:T(8,128)(2,1)}, bf16[4,64,256]{2,1,0:T(8,128)(2...) custom-call(s32[3]{0:T(128)} %pad_add_fusion.info_ref, ...), custom_call_target="tpu_custom_call" | custom-call | flops 5368709120 | bytes 1048576 | tf_op jit(solution)/shard_map/pallas_call | solution.py:231
  391.1 5.5 collective-permute-done.36.refs_3_
  397.5 2.7 shard_map.221.refs_11_
  400.2 4.5 all-to-all-start.8
  407.0 25.9 %shard_map.222 = (bf16[4,64,256]{2,1,0:T(8,128)(2,1)}, bf16[4,64,256]{2,1,0:T(8,128)(2,1)}, bf16[4,64,256]{2,1,0:T(8,128)(2,1)}, bf16[4,64,256]{2,1,0:T(8,128)(2...) custom-call(s32[3]{0:T(128)} %pad_add_fusion.info_ref, ...), custom_call_target="tpu_custom_call" | custom-call | flops 5368709120 | bytes 1048576 | tf_op jit(solution)/shard_map/pallas_call | solution.py:231
  435.9 5.1 all-to-all-start.9
  445.2 3.3 collective-permute-done.42.refs_1_
  453.3 17.5 %all_to_all.61.refs_3_ = bf16[4,384,128]{2,1,0:T(8,128)(2,1)} all-to-all(bf16[4,384,128]{2,1,0:T(8,128)(2,1)} %shard_map.224), channel_id=1, replica_groups=mesh['f'=2,'g'=4,'x'=2,'c'=2] {'g'}, dimensions={0} | all-to-all | bytes 786432 | tf_op jit(solution)/shard_map/all_to_all | solution.py:657
  470.9 13.3 %shard_map.225 = (bf16[512,768]{1,0:T(8,128)(2,1)}, bf16[4,1792,128]{2,1,0:T(8,128)(2,1)}, bf16[4,1792,128]{2,1,0:T(8,128)(2,1)}) custom-call(s32[3]{0:T(128)} %pad_add_fusion.info_ref, bf16[512,768]{1,0:T(8,128)(2,1)} %bitcast.84, f32[768]{0:T(1024)} %gain_ref.5, f32[768]{0:T(1024)} %shift_ref.5, bf16[768,2304]{1,0:T(8,128)(2,1)} %w_ref.3, ...), custom_call_target="tpu_custom_call" | custom-call | flops 393216 | bytes 786 | tf_op jit(solution)/shard_map/pallas_call | solution.py:488
  484.2 4.0 collective-permute-done.45
  492.3 10.9 %collective-permute-done.48 = bf16[2,2,448,128]{3,2,0,1:T(8,128)(2,1)S(1)} collective-permute-done((bf16[2,2,448,128]{3,2,0,1:T(8,128)(2,1)S(1)}, bf16[2,2,448,128]{3,2,0,1:T(8,128)(2,1)S(1)}, u32[]{:S(2)}, u32[]{:S(2)}) %collective-permute-start.48) | collective-permute-done | bytes 458784 | tf_op jit(solution)/shard_map/ppermute | solution.py:402
  505.4 5.0 collective-permute-done.49
  511.9 18.2 %all_to_all.62 = bf16[4,448,128]{2,1,0:T(8,128)(2,1)S(1)} all-to-all(bf16[4,448,128]{2,1,0:T(8,128)(2,1)S(1)} %pad_maximum_fusion), channel_id=1, replica_groups=mesh['f'=2,'g'=4,'x'=2,'c'=2] {'g'}, dimensions={0} | all-to-all | bytes 917504 | tf_op jit(solution)/shard_map/all_to_all | solution.py:657
  535.8 4.9 collective-permute-done.52
  (276 shorter events, 83.9 us)
Async XLA Ops:
  39.7 39.6 %all-to-all-start = ((bf16[4,1536,128]{2,1,0:T(8,128)(2,1)}), bf16[4,1536,128]{2,1,0:T(8,128)(2,1)S(1)}, u32[]{:S(2)}, u32[]{:S(2)}) async-start(bf16[4,1536,128]{2,1,0:T(8,128)(2,1)} %get-tuple-element.143), calls=%async_computation | async-start | bytes 3145728 | tf_op jit(solution)/shard_map/all_to_all | solution.py:657
  44.1 35.4 %collective-permute-start = (bf16[4,2,256,128]{3,2,1,0:T(8,128)(2,1)}, bf16[4,2,256,128]{3,2,1,0:T(8,128)(2,1)}, u32[]{:S(2)}, u32[]{:S(2)}) collective-permute-start(bf16[4,2,256,128]{3,2,1,0:T(8,128)(2,1)} %bitcast.3), channel_id=1, source_target_pairs={{0,16},{16,0},{1,17},{17,1},{2,18},{18,2},{3,19},{19,3},{4,20},{20... | collective-permute-start | bytes 1572872 | tf_op jit(solution)/shard_map/ppermute | solution.py:402
  45.6 33.8 %collective-permute-start.1 = (bf16[4,4,64,128]{3,2,1,0:T(8,128)(2,1)S(1)}, bf16[4,4,64,128]{3,2,1,0:T(8,128)(2,1)}, u32[]{:S(2)}, u32[]{:S(2)}) collective-permute-start(bf16[4,4,64,128]{3,2,1,0:T(8,128)(2,1)S(1)} %bitcast.102), channel_id=1, source_target_pairs={{0,2},{1,3},{2,0},{3,1},{4,6},{5,7},{6,4},{7,5},{8,10},{9,11},{10,... | collective-permute-start | bytes 786440 | tf_op jit(solution)/shard_map/ppermute | solution.py:665
  47.2 32.3 %collective-permute-start.2 = (bf16[4,4,64,128]{3,2,1,0:T(8,128)(2,1)S(1)}, bf16[4,4,64,128]{3,2,1,0:T(8,128)(2,1)}, u32[]{:S(2)}, u32[]{:S(2)}) collective-permute-start(bf16[4,4,64,128]{3,2,1,0:T(8,128)(2,1)S(1)} %bitcast.103), channel_id=1, source_target_pairs={{0,1},{1,0},{2,3},{3,2},{4,5},{5,4},{6,7},{7,6},{8,9},{9,8},{10,11... | collective-permute-start | bytes 786440 | tf_op jit(solution)/shard_map/ppermute | solution.py:665
  47.2 32.3 %collective-permute-start.3 = (bf16[4,4,64,128]{3,2,1,0:T(8,128)(2,1)S(1)}, bf16[4,4,64,128]{3,2,1,0:T(8,128)(2,1)}, u32[]{:S(2)}, u32[]{:S(2)}) collective-permute-start(bf16[4,4,64,128]{3,2,1,0:T(8,128)(2,1)S(1)} %bitcast.104), channel_id=1, source_target_pairs={{0,3},{1,2},{2,1},{3,0},{4,7},{5,6},{6,5},{7,4},{8,11},{9,10},{10,... | collective-permute-start | bytes 786440 | tf_op jit(solution)/shard_map/ppermute | solution.py:665
  79.5 24.4 %collective-permute-start.4 = (bf16[4,4,256,128]{3,2,1,0:T(8,128)(2,1)S(1)}, bf16[4,4,256,128]{3,2,1,0:T(8,128)(2,1)S(1)}, u32[]{:S(2)}, u32[]{:S(2)}) collective-permute-start(bf16[4,4,256,128]{3,2,1,0:T(8,128)(2,1)S(1)} %bitcast.73), channel_id=1, source_target_pairs={{0,16},{16,0},{1,17},{17,1},{2,18},{18,2},{3,19},{19,3},{4,20},{20... | collective-permute-start | bytes 3145736 | tf_op jit(solution)/shard_map/ppermute | solution.py:402
  81.1 21.0 %collective-permute-start.5 = (bf16[4,8,64,128]{3,2,1,0:T(8,128)(2,1)S(1)}, bf16[4,8,64,128]{3,2,1,0:T(8,128)(2,1)}, u32[]{:S(2)}, u32[]{:S(2)}) collective-permute-start(bf16[4,8,64,128]{3,2,1,0:T(8,128)(2,1)S(1)} %bitcast.85), channel_id=1, source_target_pairs={{0,2},{1,3},{2,0},{3,1},{4,6},{5,7},{6,4},{7,5},{8,10},{9,11},{10,... | collective-permute-start | bytes 1572872 | tf_op jit(solution)/shard_map/ppermute | solution.py:665
  82.6 19.5 %collective-permute-start.6 = (bf16[4,8,64,128]{3,2,1,0:T(8,128)(2,1)S(1)}, bf16[4,8,64,128]{3,2,1,0:T(8,128)(2,1)}, u32[]{:S(2)}, u32[]{:S(2)}) collective-permute-start(bf16[4,8,64,128]{3,2,1,0:T(8,128)(2,1)S(1)} %bitcast.86), channel_id=1, source_target_pairs={{0,1},{1,0},{2,3},{3,2},{4,5},{5,4},{6,7},{7,6},{8,9},{9,8},{10,11... | collective-permute-start | bytes 1572872 | tf_op jit(solution)/shard_map/ppermute | solution.py:665
  82.6 21.3 %collective-permute-start.7 = (bf16[4,8,64,128]{3,2,1,0:T(8,128)(2,1)S(1)}, bf16[4,8,64,128]{3,2,1,0:T(8,128)(2,1)}, u32[]{:S(2)}, u32[]{:S(2)}) collective-permute-start(bf16[4,8,64,128]{3,2,1,0:T(8,128)(2,1)S(1)} %bitcast.87), channel_id=1, source_target_pairs={{0,3},{1,2},{2,1},{3,0},{4,7},{5,6},{6,5},{7,4},{8,11},{9,10},{10,... | collective-permute-start | bytes 1572872 | tf_op jit(solution)/shard_map/ppermute | solution.py:665
  103.9 10.8 %collective-permute-start.8 = (bf16[4,80,512]{2,1,0:T(8,128)(2,1)}, bf16[4,80,512]{2,1,0:T(8,128)(2,1)S(1)}, u32[]{:S(2)}, u32[]{:S(2)}) collective-permute-start(bf16[4,80,512]{2,1,0:T(8,128)(2,1)} %get-tuple-element.159), channel_id=1, source_target_pairs={{0,2},{1,3},{2,0},{3,1},{4,6},{5,7},{6,4},{7,5},{8,10},{9,11},{10,... | collective-permute-start | bytes 983048 | tf_op jit(solution)/shard_map/ppermute | solution.py:665
  106.1 15.6 %collective-permute-start.10 = (bf16[4,80,512]{2,1,0:T(8,128)(2,1)}, bf16[4,80,512]{2,1,0:T(8,128)(2,1)S(1)}, u32[]{:S(2)}, u32[]{:S(2)}) collective-permute-start(bf16[4,80,512]{2,1,0:T(8,128)(2,1)} %get-tuple-element.161), channel_id=1, source_target_pairs={{0,3},{1,2},{2,1},{3,0},{4,7},{5,6},{6,5},{7,4},{8,11},{9,10},{10,... | collective-permute-start | bytes 983048 | tf_op jit(solution)/shard_map/ppermute | solution.py:665
  124.8 35.3 %all-to-all-start.2 = ((bf16[4,64,512]{2,1,0:T(8,128)(2,1)}), bf16[4,64,512]{2,1,0:T(8,128)(2,1)S(1)}, u32[]{:S(2)}, u32[]{:S(2)}) async-start(bf16[4,64,512]{2,1,0:T(8,128)(2,1)} %get-tuple-element.162.refs_11_), calls=%async_computation.2 | async-start | bytes 524288 | tf_op jit(solution)/shard_map/all_to_all | solution.py:657
  140.7 10.8 %collective-permute-start.11 = (bf16[4,80,512]{2,1,0:T(8,128)(2,1)}, bf16[4,80,512]{2,1,0:T(8,128)(2,1)S(1)}, u32[]{:S(2)}, u32[]{:S(2)}) collective-permute-start(bf16[4,80,512]{2,1,0:T(8,128)(2,1)} %get-tuple-element.170), channel_id=1, source_target_pairs={{0,2},{1,3},{2,0},{3,1},{4,6},{5,7},{6,4},{7,5},{8,10},{9,11},{10,... | collective-permute-start | bytes 983048 | tf_op jit(solution)/shard_map/ppermute | solution.py:665
  142.1 14.8 %collective-permute-start.13 = (bf16[4,80,512]{2,1,0:T(8,128)(2,1)}, bf16[4,80,512]{2,1,0:T(8,128)(2,1)S(1)}, u32[]{:S(2)}, u32[]{:S(2)}) collective-permute-start(bf16[4,80,512]{2,1,0:T(8,128)(2,1)} %get-tuple-element.172), channel_id=1, source_target_pairs={{0,3},{1,2},{2,1},{3,0},{4,7},{5,6},{6,5},{7,4},{8,11},{9,10},{10,... | collective-permute-start | bytes 983048 | tf_op jit(solution)/shard_map/ppermute | solution.py:665
  160.1 22.0 %all-to-all-start.3 = ((bf16[4,64,512]{2,1,0:T(8,128)(2,1)}), bf16[4,64,512]{2,1,0:T(8,128)(2,1)S(1)}, u32[]{:S(2)}, u32[]{:S(2)}) async-start(bf16[4,64,512]{2,1,0:T(8,128)(2,1)} %get-tuple-element.174.refs_7_), calls=%async_computation.3 | async-start | bytes 524288 | tf_op jit(solution)/shard_map/all_to_all | solution.py:657
  164.6 14.6 %collective-permute-start.14 = (bf16[4,80,256]{2,1,0:T(8,128)(2,1)S(1)}, bf16[4,80,256]{2,1,0:T(8,128)(2,1)S(1)}, u32[]{:S(2)}, u32[]{:S(2)}) collective-permute-start(bf16[4,80,256]{2,1,0:T(8,128)(2,1)S(1)} %copy-done.62), channel_id=1, source_target_pairs={{0,2},{1,3},{2,0},{3,1},{4,6},{5,7},{6,4},{7,5},{8,10},{9,11},{10,... | collective-permute-start | bytes 491528 | tf_op jit(solution)/shard_map/ppermute | solution.py:665
  165.5 13.7 %collective-permute-start.15 = (bf16[4,80,256]{2,1,0:T(8,128)(2,1)S(1)}, bf16[4,80,256]{2,1,0:T(8,128)(2,1)S(1)}, u32[]{:S(2)}, u32[]{:S(2)}) collective-permute-start(bf16[4,80,256]{2,1,0:T(8,128)(2,1)S(1)} %copy-done.61), channel_id=1, source_target_pairs={{0,1},{1,0},{2,3},{3,2},{4,5},{5,4},{6,7},{7,6},{8,9},{9,8},{10,11... | collective-permute-start | bytes 491528 | tf_op jit(solution)/shard_map/ppermute | solution.py:665
  166.1 13.1 %collective-permute-start.16 = (bf16[4,80,256]{2,1,0:T(8,128)(2,1)S(1)}, bf16[4,80,256]{2,1,0:T(8,128)(2,1)S(1)}, u32[]{:S(2)}, u32[]{:S(2)}) collective-permute-start(bf16[4,80,256]{2,1,0:T(8,128)(2,1)S(1)} %copy-done.60), channel_id=1, source_target_pairs={{0,3},{1,2},{2,1},{3,0},{4,7},{5,6},{6,5},{7,4},{8,11},{9,10},{10,... | collective-permute-start | bytes 491528 | tf_op jit(solution)/shard_map/ppermute | solution.py:665
  182.1 16.5 %all-to-all-start.4 = ((bf16[4,64,256]{2,1,0:T(8,128)(2,1)}), bf16[4,64,256]{2,1,0:T(8,128)(2,1)S(1)}, u32[]{:S(2)}, u32[]{:S(2)}) async-start(bf16[4,64,256]{2,1,0:T(8,128)(2,1)} %get-tuple-element.181), calls=%async_computation.4 | async-start | bytes 262144 | tf_op jit(solution)/shard_map/all_to_all | solution.py:657
  198.6 11.3 %all-to-all-start.5 = ((bf16[4,64,256]{2,1,0:T(8,128)(2,1)}), bf16[4,64,256]{2,1,0:T(8,128)(2,1)S(1)}, u32[]{:S(2)}, u32[]{:S(2)}) async-start(bf16[4,64,256]{2,1,0:T(8,128)(2,1)} %get-tuple-element.191), calls=%async_computation.5 | async-start | bytes 262144 | tf_op jit(solution)/shard_map/all_to_all | solution.py:657
  233.1 26.6 %all-to-all-start.6 = ((bf16[4,192,512]{2,1,0:T(8,128)(2,1)}), bf16[4,192,512]{2,1,0:T(8,128)(2,1)S(1)}, u32[]{:S(2)}, u32[]{:S(2)}) async-start(bf16[4,192,512]{2,1,0:T(8,128)(2,1)} %get-tuple-element.194), calls=%async_computation.6 | async-start | bytes 1572864 | tf_op jit(solution)/shard_map/all_to_all | solution.py:657
  236.6 50.8 %reduce-scatter.6.cloned.1.call-start = ((), (), s32[]{:S(2)}) async-start(), calls=%async_computation.15 | async-start | bytes 21430272 | tf_op jit(solution)/shard_map/reduce_scatter | solution.py:857
  263.4 220.8 %reduce-scatter.10.cloned.1.call-start = ((), (), s32[]{:S(2)}) async-start(), calls=%async_computation.17 | async-start | bytes 8929280
  264.3 9.6 %collective-permute-start.20 = (bf16[4,80,512]{2,1,0:T(8,128)(2,1)S(1)}, bf16[4,80,512]{2,1,0:T(8,128)(2,1)S(1)}, u32[]{:S(2)}, u32[]{:S(2)}) collective-permute-start(bf16[4,80,512]{2,1,0:T(8,128)(2,1)S(1)} %copy-done.51), channel_id=1, source_target_pairs={{0,2},{2,0},{1,3},{3,1},{4,6},{6,4},{5,7},{7,5},{8,10},{10,8},{9,1... | collective-permute-start | bytes 983048 | tf_op jit(solution)/shard_map/ppermute | solution.py:402
  287.5 28.2 %collective-permute-start.23 = (bf16[4,80,512]{2,1,0:T(8,128)(2,1)S(1)}, bf16[4,80,512]{2,1,0:T(8,128)(2,1)S(1)}, u32[]{:S(2)}, u32[]{:S(2)}) collective-permute-start(bf16[4,80,512]{2,1,0:T(8,128)(2,1)S(1)} %copy-done.44), channel_id=1, source_target_pairs={{0,2},{1,3},{2,0},{3,1},{4,6},{5,7},{6,4},{7,5},{8,10},{9,11},{10,... | collective-permute-start | bytes 983048 | tf_op jit(solution)/shard_map/ppermute | solution.py:665
  289.3 26.4 %collective-permute-start.24 = (bf16[4,80,512]{2,1,0:T(8,128)(2,1)S(1)}, bf16[4,80,512]{2,1,0:T(8,128)(2,1)S(1)}, u32[]{:S(2)}, u32[]{:S(2)}) collective-permute-start(bf16[4,80,512]{2,1,0:T(8,128)(2,1)S(1)} %copy-done.44), channel_id=1, source_target_pairs={{0,1},{1,0},{2,3},{3,2},{4,5},{5,4},{6,7},{7,6},{8,9},{9,8},{10,11... | collective-permute-start | bytes 983048 | tf_op jit(solution)/shard_map/ppermute | solution.py:665
  289.3 26.4 %collective-permute-start.25 = (bf16[4,80,512]{2,1,0:T(8,128)(2,1)S(1)}, bf16[4,80,512]{2,1,0:T(8,128)(2,1)S(1)}, u32[]{:S(2)}, u32[]{:S(2)}) collective-permute-start(bf16[4,80,512]{2,1,0:T(8,128)(2,1)S(1)} %copy-done.44), channel_id=1, source_target_pairs={{0,3},{1,2},{2,1},{3,0},{4,7},{5,6},{6,5},{7,4},{8,11},{9,10},{10,... | collective-permute-start | bytes 983048 | tf_op jit(solution)/shard_map/ppermute | solution.py:665
  317.1 23.2 %collective-permute-start.26 = (bf16[4,2,256,128]{3,2,1,0:T(8,128)(2,1)S(1)}, bf16[4,2,256,128]{3,2,1,0:T(8,128)(2,1)S(1)}, u32[]{:S(2)}, u32[]{:S(2)}) collective-permute-start(bf16[4,2,256,128]{3,2,1,0:T(8,128)(2,1)S(1)} %bitcast.124), channel_id=1, source_target_pairs={{0,16},{16,0},{1,17},{17,1},{2,18},{18,2},{3,19},{19,3},{4,20},{20... | collective-permute-start | bytes 1572872 | tf_op jit(solution)/shard_map/ppermute | solution.py:402
  318.8 11.4 %collective-permute-start.27 = (bf16[4,64,512]{2,1,0:T(8,128)(2,1)S(1)}, bf16[4,64,512]{2,1,0:T(8,128)(2,1)S(1)}, u32[]{:S(2)}, u32[]{:S(2)}) collective-permute-start(bf16[4,64,512]{2,1,0:T(8,128)(2,1)S(1)} %copy-done.57), channel_id=1, source_target_pairs={{0,2},{1,3},{2,0},{3,1},{4,6},{5,7},{6,4},{7,5},{8,10},{9,11},{10,... | collective-permute-start | bytes 786440 | tf_op jit(solution)/shard_map/ppermute | solution.py:665
  320.3 10.0 %collective-permute-start.28 = (bf16[4,64,512]{2,1,0:T(8,128)(2,1)S(1)}, bf16[4,64,512]{2,1,0:T(8,128)(2,1)S(1)}, u32[]{:S(2)}, u32[]{:S(2)}) collective-permute-start(bf16[4,64,512]{2,1,0:T(8,128)(2,1)S(1)} %copy-done.58), channel_id=1, source_target_pairs={{0,1},{1,0},{2,3},{3,2},{4,5},{5,4},{6,7},{7,6},{8,9},{9,8},{10,11... | collective-permute-start | bytes 786440 | tf_op jit(solution)/shard_map/ppermute | solution.py:665
  320.3 20.0 %collective-permute-start.29 = (bf16[4,64,512]{2,1,0:T(8,128)(2,1)S(1)}, bf16[4,64,512]{2,1,0:T(8,128)(2,1)S(1)}, u32[]{:S(2)}, u32[]{:S(2)}) collective-permute-start(bf16[4,64,512]{2,1,0:T(8,128)(2,1)S(1)} %copy-done.59), channel_id=1, source_target_pairs={{0,3},{1,2},{2,1},{3,0},{4,7},{5,6},{6,5},{7,4},{8,11},{9,10},{10,... | collective-permute-start | bytes 786440 | tf_op jit(solution)/shard_map/ppermute | solution.py:665
  343.8 56.4 %all-to-all-start.7 = ((bf16[4,768,128]{2,1,0:T(8,128)(2,1)}), bf16[4,768,128]{2,1,0:T(8,128)(2,1)S(1)}, u32[]{:S(2)}, u32[]{:S(2)}) async-start(bf16[4,768,128]{2,1,0:T(8,128)(2,1)} %shard_map.218.refs_17_), calls=%async_computation.8 | async-start | bytes 1572864 | tf_op jit(solution)/shard_map/all_to_all | solution.py:657
  348.4 28.2 %collective-permute-start.30 = (bf16[4,80,512]{2,1,0:T(8,128)(2,1)S(1)}, bf16[4,80,512]{2,1,0:T(8,128)(2,1)S(1)}, u32[]{:S(2)}, u32[]{:S(2)}) collective-permute-start(bf16[4,80,512]{2,1,0:T(8,128)(2,1)S(1)} %copy-done.43), channel_id=1, source_target_pairs={{0,2},{1,3},{2,0},{3,1},{4,6},{5,7},{6,4},{7,5},{8,10},{9,11},{10,... | collective-permute-start | bytes 983048 | tf_op jit(solution)/shard_map/ppermute | solution.py:665
  348.4 28.2 %collective-permute-start.31 = (bf16[4,80,512]{2,1,0:T(8,128)(2,1)S(1)}, bf16[4,80,512]{2,1,0:T(8,128)(2,1)S(1)}, u32[]{:S(2)}, u32[]{:S(2)}) collective-permute-start(bf16[4,80,512]{2,1,0:T(8,128)(2,1)S(1)} %copy-done.43), channel_id=1, source_target_pairs={{0,1},{1,0},{2,3},{3,2},{4,5},{5,4},{6,7},{7,6},{8,9},{9,8},{10,11... | collective-permute-start | bytes 983048 | tf_op jit(solution)/shard_map/ppermute | solution.py:665
  350.6 29.1 %collective-permute-start.32 = (bf16[4,80,512]{2,1,0:T(8,128)(2,1)S(1)}, bf16[4,80,512]{2,1,0:T(8,128)(2,1)S(1)}, u32[]{:S(2)}, u32[]{:S(2)}) collective-permute-start(bf16[4,80,512]{2,1,0:T(8,128)(2,1)S(1)} %copy-done.43), channel_id=1, source_target_pairs={{0,3},{1,2},{2,1},{3,0},{4,7},{5,6},{6,5},{7,4},{8,11},{9,10},{10,... | collective-permute-start | bytes 983048 | tf_op jit(solution)/shard_map/ppermute | solution.py:665
  379.8 16.9 %collective-permute-start.33 = (bf16[4,2,256,128]{3,2,1,0:T(8,128)(2,1)}, bf16[4,2,256,128]{3,2,1,0:T(8,128)(2,1)S(1)}, u32[]{:S(2)}, u32[]{:S(2)}) collective-permute-start(bf16[4,2,256,128]{3,2,1,0:T(8,128)(2,1)} %bitcast.123), channel_id=1, source_target_pairs={{0,16},{16,0},{1,17},{17,1},{2,18},{18,2},{3,19},{19,3},{4,20},{20... | collective-permute-start | bytes 1572872 | tf_op jit(solution)/shard_map/ppermute | solution.py:402
  379.8 11.3 %collective-permute-start.34 = (bf16[4,64,512]{2,1,0:T(8,128)(2,1)}, bf16[4,64,512]{2,1,0:T(8,128)(2,1)S(1)}, u32[]{:S(2)}, u32[]{:S(2)}) collective-permute-start(bf16[4,64,512]{2,1,0:T(8,128)(2,1)} %get-tuple-element.251), channel_id=1, source_target_pairs={{0,2},{1,3},{2,0},{3,1},{4,6},{5,7},{6,4},{7,5},{8,10},{9,11},{10,... | collective-permute-start | bytes 786440 | tf_op jit(solution)/shard_map/ppermute | solution.py:665
  381.1 10.0 %collective-permute-start.35 = (bf16[4,64,512]{2,1,0:T(8,128)(2,1)}, bf16[4,64,512]{2,1,0:T(8,128)(2,1)S(1)}, u32[]{:S(2)}, u32[]{:S(2)}) collective-permute-start(bf16[4,64,512]{2,1,0:T(8,128)(2,1)} %get-tuple-element.252), channel_id=1, source_target_pairs={{0,1},{1,0},{2,3},{3,2},{4,5},{5,4},{6,7},{7,6},{8,9},{9,8},{10,11... | collective-permute-start | bytes 786440 | tf_op jit(solution)/shard_map/ppermute | solution.py:665
  381.1 15.6 %collective-permute-start.36 = (bf16[4,64,512]{2,1,0:T(8,128)(2,1)}, bf16[4,64,512]{2,1,0:T(8,128)(2,1)S(1)}, u32[]{:S(2)}, u32[]{:S(2)}) collective-permute-start(bf16[4,64,512]{2,1,0:T(8,128)(2,1)} %get-tuple-element.253), channel_id=1, source_target_pairs={{0,3},{1,2},{2,1},{3,0},{4,7},{5,6},{6,5},{7,4},{8,11},{9,10},{10,... | collective-permute-start | bytes 786440 | tf_op jit(solution)/shard_map/ppermute | solution.py:665
  400.2 35.6 %all-to-all-start.8 = ((bf16[4,768,128]{2,1,0:T(8,128)(2,1)}), bf16[4,768,128]{2,1,0:T(8,128)(2,1)S(1)}, u32[]{:S(2)}, u32[]{:S(2)}) async-start(bf16[4,768,128]{2,1,0:T(8,128)(2,1)} %shard_map.221.refs_11_), calls=%async_computation.9 | async-start | bytes 1572864 | tf_op jit(solution)/shard_map/all_to_all | solution.py:657
  404.7 28.2 %collective-permute-start.37 = (bf16[4,1,256,128]{3,2,0,1:T(8,128)(2,1)S(1)}, bf16[4,1,256,128]{3,2,0,1:T(8,128)(2,1)S(1)}, u32[]{:S(2)}, u32[]{:S(2)}) collective-permute-start(bf16[4,1,256,128]{3,2,0,1:T(8,128)(2,1)S(1)} %bitcast.125), channel_id=1, source_target_pairs={{0,16},{16,0},{1,17},{17,1},{2,18},{18,2},{3,19},{19,3},{4,20},{20... | collective-permute-start | bytes 786440 | tf_op jit(solution)/shard_map/ppermute | solution.py:402
  404.7 28.2 %collective-permute-start.38 = (bf16[4,64,256]{2,1,0:T(8,128)(2,1)S(1)}, bf16[4,64,256]{2,1,0:T(8,128)(2,1)S(1)}, u32[]{:S(2)}, u32[]{:S(2)}) collective-permute-start(bf16[4,64,256]{2,1,0:T(8,128)(2,1)S(1)} %copy-done.66), channel_id=1, source_target_pairs={{0,2},{1,3},{2,0},{3,1},{4,6},{5,7},{6,4},{7,5},{8,10},{9,11},{10,... | collective-permute-start | bytes 393224 | tf_op jit(solution)/shard_map/ppermute | solution.py:665
  406.4 26.6 %collective-permute-start.39 = (bf16[4,64,256]{2,1,0:T(8,128)(2,1)S(1)}, bf16[4,64,256]{2,1,0:T(8,128)(2,1)S(1)}, u32[]{:S(2)}, u32[]{:S(2)}) collective-permute-start(bf16[4,64,256]{2,1,0:T(8,128)(2,1)S(1)} %copy-done.64), channel_id=1, source_target_pairs={{0,1},{1,0},{2,3},{3,2},{4,5},{5,4},{6,7},{7,6},{8,9},{9,8},{10,11... | collective-permute-start | bytes 393224 | tf_op jit(solution)/shard_map/ppermute | solution.py:665
  406.8 26.1 %collective-permute-start.40 = (bf16[4,64,256]{2,1,0:T(8,128)(2,1)S(1)}, bf16[4,64,256]{2,1,0:T(8,128)(2,1)S(1)}, u32[]{:S(2)}, u32[]{:S(2)}) collective-permute-start(bf16[4,64,256]{2,1,0:T(8,128)(2,1)S(1)} %copy-done.63), channel_id=1, source_target_pairs={{0,3},{1,2},{2,1},{3,0},{4,7},{5,6},{6,5},{7,4},{8,11},{9,10},{10,... | collective-permute-start | bytes 393224 | tf_op jit(solution)/shard_map/ppermute | solution.py:665
  435.9 17.4 %all-to-all-start.9 = ((bf16[4,384,128]{2,1,0:T(8,128)(2,1)}), bf16[4,384,128]{2,1,0:T(8,128)(2,1)S(1)}, u32[]{:S(2)}, u32[]{:S(2)}) async-start(bf16[4,384,128]{2,1,0:T(8,128)(2,1)} %shard_map.223), calls=%async_computation.10 | async-start | bytes 786432 | tf_op jit(solution)/shard_map/all_to_all | solution.py:657
  441.0 89.2 %reduce-scatter.8.cloned.1.call-start = ((), (), s32[]{:S(2)}) async-start(), calls=%async_computation.16 | async-start | bytes 2232320 | tf_op jit(solution)/shard_map/reduce_scatter | solution.py:899
  490.4 12.7 %collective-permute-start.48 = (bf16[2,2,448,128]{3,2,0,1:T(8,128)(2,1)S(1)}, bf16[2,2,448,128]{3,2,0,1:T(8,128)(2,1)S(1)}, u32[]{:S(2)}, u32[]{:S(2)}) collective-permute-start(bf16[2,2,448,128]{3,2,0,1:T(8,128)(2,1)S(1)} %bitcast.100), channel_id=1, source_target_pairs={{0,16},{16,0},{1,17},{17,1},{2,18},{18,2},{3,19},{19,3},{4,20},{20... | collective-permute-start | bytes 1376264 | tf_op jit(solution)/shard_map/ppermute | solution.py:402
  490.7 14.2 %collective-permute-start.46 = (bf16[2,2,448,128]{3,2,0,1:T(8,128)(2,1)S(1)}, bf16[2,2,448,128]{3,2,0,1:T(8,128)(2,1)S(1)}, u32[]{:S(2)}, u32[]{:S(2)}) collective-permute-start(bf16[2,2,448,128]{3,2,0,1:T(8,128)(2,1)S(1)} %bitcast.101), channel_id=1, source_target_pairs={{0,2},{2,0},{1,3},{3,1},{4,6},{6,4},{5,7},{7,5},{8,10},{10,8},{9,1... | collective-permute-start | bytes 1376264 | tf_op jit(solution)/shard_map/ppermute | solution.py:402
  (86 other events, 635.0 us)
Sparse Core Ops, SparseCore 0:
  263.5 23.9 reduce-scatter.5
  315.9 106.5 reduce-scatter.9
  484.3 38.7 reduce-scatter.7
